TPU v7x, 128 devices: a whole 4x4x4 slice. The times are simulated.
128 devices in a mesh: dp: 4 (over z_lo, core), tm: 8 (over x, z_hi), head: 4 (over y).
Axes of the slice: x: 4, y: 4, z: 4 (z_hi: 2, z_lo: 2; z = z_hi * 2 + z_lo), core: 2. Of those that a mesh axis runs over, the one named last changes fastest.
Arguments:
- frames: bfloat16 [4, 3072, 1536], P('dp', 'tm')
- projections: bfloat16 [4, 1536, 1536], P(None, None, 'head')
- kernel: bfloat16 [32, 1536], replicated, may hold values from -1 to 1
- pattern: int32 [4, 48, 12], P('dp', 'tm'), may hold values from -1 to 47, as said below
- cotangent: bfloat16 [4, 3072, 1536], P('dp', 'tm'), may hold values from -0.0546875 to 0.0546875
Outputs:
- encoded: bfloat16 [4, 3072, 1536], P('dp', 'tm')
- proj_grad: float32 [4, 1536, 1536], P(None, ('dp', 'tm'), 'head')
- kernel_grad: float32 [32, 1536], P(('dp', 'tm'))
Inputs may be any that keep to these rules, and one draw needn't show every extreme that they name: `pattern`: in each row the strided key blocks come first: phase + j * 4 for j = 0, 1, ..., one phase below 4 for the row, 1 to 12 of them; the remaining entries are -1.
All inputs are finite; a program needn't handle non-finite values.
Results may differ from a plain program's by a relative error of at most 0.04.
Values may be sent and summed in bfloat16 or wider, within the bound.
A program may use at most 128 MiB of HBM per device.

v0:
```python
import jax
import jax.numpy as jnp
from jax import lax
from jax.sharding import PartitionSpec as P

HD = 96
BLK = 64
KW = 32


def extended_2(array, sides, width):
    for axis, dim in sides:
        peers, length = (lax.axis_size(axis), array.shape[dim])
        up = [(i, (i + 1) % peers) for i in range(peers - 1)]
        down = [(j, i) for i, j in up]
        last = lax.slice_in_dim(array, length - width, length, axis=dim)
        first = lax.slice_in_dim(array, 0, width, axis=dim)
        before = lax.ppermute(last, axis, up)
        after = lax.ppermute(first, axis, down)
        array = jnp.concatenate([before, array, after], axis=dim)
    return array


def key_lists(pattern, first_block, nblocks):
    query_count = pattern.shape[0]
    query_block = first_block + jnp.arange(query_count, dtype=jnp.int32)
    band_blocks = query_block[:, None] + jnp.arange(-1, 2, dtype=jnp.int32)[None, :]
    band_live = (band_blocks >= 0) & (band_blocks < nblocks)
    far_live = (pattern >= 0) & (jnp.abs(pattern - query_block[:, None]) > 1)
    listed = jnp.clip(jnp.concatenate([band_blocks, pattern], axis=1), 0, nblocks - 1)
    live_mask = jnp.concatenate([band_live, far_live], axis=1)
    return (listed, live_mask)


def gather_blocks(source, listed, block_len, head_dim):
    head_count = source.shape[1] // head_dim
    gathered = source.reshape(-1, block_len, head_count, head_dim)[listed]
    return gathered.reshape(listed.shape[0], listed.shape[1] * block_len, head_count, head_dim)


def masked_scores(query_tiles, key_tiles, live_mask, block_len):
    score_scale = query_tiles.shape[-1] ** (-0.5)
    scores = (
        jnp.einsum("qthd,qkhd->qhtk", query_tiles, key_tiles, preferred_element_type=jnp.float32)
        * score_scale
    )
    column_live = jnp.repeat(live_mask, block_len, axis=1)[:, None, None, :]
    return (jnp.where(column_live, scores, -1e30), column_live)


def attend(queries, key_rows, values, listed, live_mask, block_len, head_dim):
    head_count = queries.shape[1] // head_dim
    query_tiles = queries.reshape(listed.shape[0], block_len, head_count, head_dim)
    key_tiles = gather_blocks(key_rows, listed, block_len, head_dim)
    value_tiles = gather_blocks(values, listed, block_len, head_dim)
    scores, column_live = masked_scores(query_tiles, key_tiles, live_mask, block_len)
    highest = jnp.max(scores, axis=-1, keepdims=True)
    logsum = highest + jnp.log(jnp.sum(jnp.exp(scores - highest), axis=-1, keepdims=True))
    weights = jnp.where(column_live, jnp.exp(scores - logsum), 0.0).astype(jnp.bfloat16)
    mixed_rows = jnp.einsum(
        "qhtk,qkhd->qthd", weights, value_tiles, preferred_element_type=jnp.float32
    ).astype(jnp.bfloat16)
    return (mixed_rows.reshape(queries.shape), logsum)


def attend_back(
    queries,
    key_rows,
    values,
    listed,
    live_mask,
    logsum,
    mixed_rows,
    grad_mixed,
    block_len,
    head_dim,
    nblocks,
):
    head_count = queries.shape[1] // head_dim
    shape_tiles = (listed.shape[0], block_len, head_count, head_dim)
    query_tiles = queries.reshape(shape_tiles)
    grad_tiles = grad_mixed.reshape(shape_tiles)
    mixed_tiles = mixed_rows.reshape(shape_tiles)
    key_tiles = gather_blocks(key_rows, listed, block_len, head_dim)
    value_tiles = gather_blocks(values, listed, block_len, head_dim)
    scores, column_live = masked_scores(query_tiles, key_tiles, live_mask, block_len)
    probabilities = jnp.where(column_live, jnp.exp(scores - logsum), 0.0)
    row_delta = jnp.einsum(
        "qthd,qthd->qht", grad_tiles, mixed_tiles, preferred_element_type=jnp.float32
    )
    grad_probs = jnp.einsum(
        "qthd,qkhd->qhtk", grad_tiles, value_tiles, preferred_element_type=jnp.float32
    )
    score_scale = head_dim ** (-0.5)
    grad_scores = (probabilities * (grad_probs - row_delta[..., None]) * score_scale).astype(
        jnp.bfloat16
    )
    grad_queries = jnp.einsum(
        "qhtk,qkhd->qthd", grad_scores, key_tiles, preferred_element_type=jnp.float32
    )
    grad_queries = grad_queries.astype(jnp.bfloat16).reshape(queries.shape)
    weights = probabilities.astype(jnp.bfloat16)
    key_terms = jnp.einsum(
        "qhtk,qthd->qkhd", grad_scores, query_tiles, preferred_element_type=jnp.float32
    )
    value_terms = jnp.einsum(
        "qhtk,qthd->qkhd", weights, grad_tiles, preferred_element_type=jnp.float32
    )
    block_ids = jnp.arange(nblocks, dtype=jnp.int32)
    onehot = (
        (listed.reshape(-1)[:, None] == block_ids[None, :]) & live_mask.reshape(-1)[:, None]
    ).astype(jnp.float32)
    tile_width = block_len * queries.shape[1]
    key_grad = jnp.dot(onehot.T, key_terms.reshape(-1, tile_width), precision=lax.Precision.HIGHEST)
    value_grad = jnp.dot(
        onehot.T, value_terms.reshape(-1, tile_width), precision=lax.Precision.HIGHEST
    )
    key_grad = key_grad.reshape(nblocks * block_len, queries.shape[1])
    value_grad = value_grad.reshape(nblocks * block_len, queries.shape[1])
    return (grad_queries, row_delta, key_grad, value_grad)


def conv_apply(residual, upstream, extended, kernel_cols, frame_count, width, half_width):
    padded = extended[:, :width]
    padded_up = extended[:, width:]
    upstream_wide = upstream.astype(jnp.float32)
    encoded = residual.astype(jnp.float32)
    back_grad = upstream_wide
    taps_grad = []
    for offset in range(2 * half_width):
        weight_row = kernel_cols[offset].astype(jnp.float32)
        shifted = padded[offset : offset + frame_count].astype(jnp.float32)
        encoded = encoded + weight_row * shifted
        back_grad = back_grad + weight_row * padded_up[
            2 * half_width - offset : 2 * half_width - offset + frame_count
        ].astype(jnp.float32)
        taps_grad.append(jnp.sum(upstream_wide * shifted, axis=0))
    return (encoded.astype(jnp.bfloat16), back_grad.astype(jnp.bfloat16), jnp.stack(taps_grad))


def shards(frames, projections, kernel, pattern, cotangent):
    source = frames[0]
    upstream = cotangent[0]
    rows_pattern = pattern[0]
    frame_count = source.shape[0]
    model_width = source.shape[1]
    head_width = projections.shape[2]
    local_blocks = frame_count // BLK
    cycle_size = lax.axis_size("tm")
    nblocks = local_blocks * cycle_size
    first_block = lax.axis_index("tm") * local_blocks
    half_width = KW // 2
    contract = (((0,), (0,)), ((), ()))
    listed, live_mask = key_lists(rows_pattern, first_block, nblocks)
    queries = jnp.dot(source, projections[0], preferred_element_type=jnp.float32).astype(
        jnp.bfloat16
    )
    key_rows = jnp.dot(source, projections[1], preferred_element_type=jnp.float32).astype(
        jnp.bfloat16
    )
    values = jnp.dot(source, projections[2], preferred_element_type=jnp.float32).astype(
        jnp.bfloat16
    )
    key_all, value_all = (
        lax.all_gather(key_rows, "tm", axis=0, tiled=True),
        lax.all_gather(values, "tm", axis=0, tiled=True),
    )
    mixed_rows, logsum = attend(queries, key_all, value_all, listed, live_mask, BLK, HD)
    output_part = lax.dot_general(
        mixed_rows, projections[3], (((1,), (1,)), ((), ())), preferred_element_type=jnp.float32
    )
    summed = lax.psum(output_part.astype(jnp.bfloat16), "head").astype(jnp.float32)
    residual = (source.astype(jnp.float32) + summed).astype(jnp.bfloat16)
    extended = extended_2(jnp.concatenate([residual, upstream], axis=1), (("tm", 0),), half_width)
    encoded, back_grad, kernel_grad = conv_apply(
        residual, upstream, extended, kernel, frame_count, model_width, half_width
    )
    grad_mixed = jnp.dot(back_grad, projections[3], preferred_element_type=jnp.float32).astype(
        jnp.bfloat16
    )
    grad_queries, row_delta, key_grad, value_grad = attend_back(
        queries,
        key_all,
        value_all,
        listed,
        live_mask,
        logsum,
        mixed_rows,
        grad_mixed,
        BLK,
        HD,
        nblocks,
    )
    key_value_terms = jnp.concatenate([key_grad, value_grad], axis=1)
    owned = lax.psum_scatter(
        key_value_terms.astype(jnp.bfloat16), "tm", scatter_dimension=0, tiled=True
    ).astype(jnp.float32)
    key_own = owned[:, :head_width].astype(jnp.bfloat16)
    value_own = owned[:, head_width:].astype(jnp.bfloat16)
    proj_grad = jnp.stack(
        [
            lax.dot_general(source, grad_queries, contract, preferred_element_type=jnp.float32),
            lax.dot_general(source, key_own, contract, preferred_element_type=jnp.float32),
            lax.dot_general(source, value_own, contract, preferred_element_type=jnp.float32),
            lax.dot_general(back_grad, mixed_rows, contract, preferred_element_type=jnp.float32),
        ]
    )
    proj_result, kernel_result = (
        lax.psum_scatter(
            proj_grad.astype(jnp.bfloat16), ("dp", "tm"), scatter_dimension=1, tiled=True
        ).astype(jnp.float32),
        lax.psum_scatter(
            kernel_grad.astype(jnp.bfloat16), ("dp", "tm"), scatter_dimension=0, tiled=True
        ).astype(jnp.float32),
    )
    return (encoded[None], proj_result, kernel_result)


def solution(mesh):
    placed = (
        P("dp", "tm", None),
        P(None, None, "head"),
        P(),
        P("dp", "tm", None),
        P("dp", "tm", None),
    )
    return jax.shard_map(
        shards,
        mesh=mesh,
        in_specs=placed,
        out_specs=(P("dp", "tm", None), P(None, ("dp", "tm"), "head"), P(("dp", "tm"), None)),
        check_vma=False,
    )
```

profile of v0, /device:TPU:1, one launch (start us, length us, event | category | flops | bytes accessed | tf_op | source)
XLA Modules:
  0.0 593.3 jit_solution(6484090319722107401)
XLA Ops:
  16.4 53.7 %all-gather.5.cloned.1.call-done = bf16[3072,384]{1,0:T(8,128)(2,1)} async-done(((bf16[384,384]{1,0:T(8,128)(2,1)}), bf16[3072,384]{1,0:T(8,128)(2,1)}) %all-gather.5.cloned.1.call-update) | async-done | bytes 2359312 | tf_op jit(solution)/shard_map/all_gather | solution.py:165
  70.0 6.9 %reshape.152 = bf16[48,64,4,96]{3,2,1,0:T(4,128)(2,1)} reshape(bf16[3072,384]{1,0:T(8,128)(2,1)} %all-gather.5.cloned.1.call-done) | data formatting | bytes 4718592 | tf_op jit(solution)/shard_map/reshape | solution.py:37
  76.9 4.5 copy.56
  81.4 47.1 %all-gather.3.cloned.1.call-done = bf16[3072,384]{1,0:T(8,128)(2,1)} async-done(((bf16[384,384]{1,0:T(8,128)(2,1)}), bf16[3072,384]{1,0:T(8,128)(2,1)}) %all-gather.3.cloned.1.call-update) | async-done | bytes 2359312 | tf_op jit(solution)/shard_map/all_gather | solution.py:166
  128.5 6.9 %reshape.149 = bf16[48,64,4,96]{3,2,1,0:T(4,128)(2,1)} reshape(bf16[3072,384]{1,0:T(8,128)(2,1)} %all-gather.3.cloned.1.call-done) | data formatting | bytes 4718592 | tf_op jit(solution)/shard_map/reshape | solution.py:37
  135.3 4.4 copy.54
  139.7 7.7 %gather_fusion = bf16[90,64,4,96]{3,1,2,0:T(8,128)(2,1)} fusion(bf16[48,64,4,96]{3,1,2,0:T(8,128)(2,1)} %copy.54, s32[1024]{0:T(1024)S(1)} %pad_clamp_fusion), kind=kCustom, calls=%fused_computation | custom fusion | bytes 8847720 | tf_op jit(solution)/shard_map/gather | solution.py:37
  147.5 7.1 %copy.55 = bf16[90,64,4,96]{3,1,0,2:T(8,128)(2,1)} copy(bf16[90,64,4,96]{3,1,2,0:T(8,128)(2,1)} %gather_fusion) | data formatting | bytes 8847360 | tf_op jit(solution)/shard_map/gather | solution.py:37
  154.6 7.7 %gather_fusion.1 = bf16[90,64,4,96]{3,1,2,0:T(8,128)(2,1)} fusion(bf16[48,64,4,96]{3,1,2,0:T(8,128)(2,1)} %copy.56, s32[1024]{0:T(1024)S(1)} %pad_clamp_fusion), kind=kCustom, calls=%fused_computation.1 | custom fusion | bytes 8847720 | tf_op jit(solution)/shard_map/gather | solution.py:37
  180.2 42.8 %all-reduce.6.cloned.1.call-done = bf16[384,1536]{1,0:T(8,128)(2,1)} async-done(((bf16[384,1536]{1,0:T(8,128)(2,1)}), bf16[384,1536]{1,0:T(8,128)(2,1)}) %all-reduce.6.cloned.1.call-update) | async-done | bytes 1179664 | tf_op jit(solution)/shard_map/psum | solution.py:172
  224.7 4.8 collective-permute-start
  231.4 5.0 collective-permute-done.1
  238.3 10.0 %add_convert_fusion = bf16[384,1536]{1,0:T(8,128)(2,1)S(1)} fusion(bf16[400,3072]{1,0:T(8,128)(2,1)S(1)} %get-tuple-element.81, bf16[400,3072]{1,0:T(8,128)(2,1)S(1)} %get-tuple-element.82, f32[1536]{0:T(1024)S(1)} %get-tuple-element.77, f32[1536]{0:T(1024)S(1)} %get-tuple-element.78, f32[1536]{0:T(1024)S(1)} %copy-done.19, f32[1536]{0:T(1024)S(1)} %copy-done.21, ...), kind=kLoop, calls=%fused_computation.189 | loop fusion | flops 57212928 | bytes 39124992 | tf_op jit(solution)/shard_map/convert_element_type | solution.py:138
  253.4 8.1 %convolution_bitcast_fusion = f32[6,960,4,96]{1,3,2,0:T(8,128)} fusion(bf16[6,64,4,96]{3,2,1,0:T(4,128)(2,1)S(1)} %reshape.155, f32[6,4,64,960]{3,2,1,0:T(8,128)} %copy-done.2, f32[6,4,64]{2,1,0:T(4,128)} %bitcast.129, pred[6,960]{1,0:T(8,128)(4,1)S(1)} %broadcast_in_dim.33), kind=kOutput, calls=%fused_computation.56 | convolution fusion | flops 290488320 | bytes 15052416 | tf_op jit(solution)/shard_map/qhtk,qthd->qkhd/dot_general | solution.py:106
  261.9 5.6 multiply_convert_fusion
  267.5 13.3 %copy.69 = f32[6,960,4,96]{3,2,1,0:T(4,128)} copy(f32[6,960,4,96]{1,3,2,0:T(8,128)} %convolution_bitcast_fusion) | data formatting | bytes 17694720 | tf_op jit(solution)/shard_map/qhtk,qthd->qkhd/transpose | solution.py:106
  280.7 15.5 %reshape.159 = f32[90,24576]{1,0:T(8,128)} reshape(f32[6,960,4,96]{3,2,1,0:T(4,128)} %copy.69) | data formatting | bytes 17694720 | tf_op jit(solution)/shard_map/reshape | solution.py:116
  296.3 9.4 %convolution_convert_fusion = bf16[48,24576]{1,0:T(8,128)(2,1)} fusion(f32[90,24576]{1,0:T(8,128)} %reshape.159, s32[90]{0:T(128)S(1)} %copy-done.84, pred[90]{0:T(512)(128)(4,1)S(1)} %copy-done.85), kind=kOutput, calls=%fused_computation.2 | convolution fusion | flops 1275208192 | bytes 11207106 | tf_op jit(solution)/shard_map/dot_general | solution.py:115
  305.6 4.5 reshape.160
  310.1 6.8 %convolution_bitcast_fusion.1 = f32[6,960,4,96]{1,3,2,0:T(8,128)} fusion(bf16[6,4,64,960]{3,2,1,0:T(8,128)(2,1)} %multiply_convert_fusion, bf16[6,64,4,96]{3,2,1,0:T(4,128)(2,1)S(1)} %reshape.151), kind=kOutput, calls=%fused_computation.57 | convolution fusion | flops 283115520 | bytes 12091392 | tf_op jit(solution)/shard_map/qhtk,qthd->qkhd/dot_general | solution.py:103
  316.9 13.3 %copy.67 = f32[6,960,4,96]{3,2,1,0:T(4,128)} copy(f32[6,960,4,96]{1,3,2,0:T(8,128)} %convolution_bitcast_fusion.1) | data formatting | bytes 17694720 | tf_op jit(solution)/shard_map/qhtk,qthd->qkhd/transpose | solution.py:103
  330.2 15.3 %reshape.157 = f32[90,24576]{1,0:T(8,128)} reshape(f32[6,960,4,96]{3,2,1,0:T(4,128)} %copy.67) | data formatting | bytes 17694720 | tf_op jit(solution)/shard_map/reshape | solution.py:114
  345.5 9.3 %convolution_convert_fusion.1 = bf16[48,24576]{1,0:T(8,128)(2,1)} fusion(f32[90,24576]{1,0:T(8,128)} %reshape.157, s32[90]{0:T(128)S(1)} %copy-done.84, pred[90]{0:T(512)(128)(4,1)S(1)} %copy-done.85), kind=kOutput, calls=%fused_computation.3 | convolution fusion | flops 1275208192 | bytes 11207106 | tf_op jit(solution)/shard_map/dot_general | solution.py:114
  354.8 4.5 reshape.158
  359.3 4.9 pad_maximum_fusion
  366.1 6.4 %fusion.86 = (bf16[1536]{0:T(1024)(128)(2,1)S(1)}, bf16[1536]{0:T(1024)(128)(2,1)S(1)}, bf16[1536]{0:T(1024)(128)(2,1)S(1)}, bf16[1536]{0:T(1024)(128)(2,1)S(1)}...) fusion(bf16[400,3072]{1,0:T(8,128)(2,1)S(1)} %get-tuple-element, ...), kind=kLoop, calls=%fused_computation.172 | loop fusion | flops 28876800 | bytes 20103168 | tf_op jit(solution)/shard_map/reduce_sum | solution.py:137
  381.5 5.1 fusion.102
  398.0 6.0 %stack.189 = bf16[32,1536]{1,0:T(8,128)(2,1)} concatenate(bf16[1,1536]{1,0:T(2,128)(2,1)} %stack.157, bf16[1,1536]{1,0:T(2,128)(2,1)} %stack.158, bf16[1,1536]{1,0:T(2,128)(2,1)} %stack.159, bf16[1,1536]{1,0:T(2,128)(2,1)} %stack.160, bf16[1,1536]{1,0:T(2,128)(2,1)} %stack.161, bf16[1,1536]{1,0:T(2,128)(2,1)} %stack.162, bf16[1,1536]{1,0:T(2,128)(2,1)} %stack.163, ...), dimensions={0} | concatenate | bytes 196608 | tf_op jit(solution)/shard_map/stack | solution.py:138
  409.1 45.4 %reduce-scatter.2.cloned.1.call-done = bf16[384,768]{1,0:T(8,128)(2,1)} async-done(((bf16[3072,768]{1,0:T(8,128)(2,1)}), bf16[384,768]{1,0:T(8,128)(2,1)}) %reduce-scatter.2.cloned.1.call-update) | async-done | bytes 589840 | tf_op jit(solution)/shard_map/reduce_scatter | solution.py:195
  461.1 8.5 %copy.71 = bf16[4,1536,384]{2,0,1:T(4,128)(2,1)} copy(bf16[4,1536,384]{1,2,0:T(8,128)(2,1)} %pad_maximum_fusion.1) | data formatting | bytes 9437184 | tf_op jit(solution)/shard_map/stack | solution.py:200
  470.6 19.9 %fusion.128 = bf16[1,384,1536]{2,1,0:T(8,128)(2,1)} fusion(f32[1536]{0:T(1024)S(1)} %copy-done.78, f32[1536]{0:T(1024)S(1)} %copy-done.80, f32[1536]{0:T(1024)S(1)} %copy-done.20, f32[1536]{0:T(1024)S(1)} %copy-done.22, f32[1536]{0:T(1024)S(1)} %copy-done.24, f32[1536]{0:T(1024)S(1)} %copy-done.26, f32[1536]{0:T(1024)S(1)} %copy-done.28, ...), kind=kLoop, calls=%fused_computation.212 | loop fusion | flops 57212928 | bytes 39124992 | tf_op jit(solution)/shard_map/broadcast_in_dim | solution.py:216
  490.5 92.2 %all-reduce.8.cloned.1.call-done = (bf16[4,1536,384]{2,0,1:T(4,128)(2,1)}, bf16[32,1536]{1,0:T(8,128)(2,1)}) async-done(((bf16[4,1536,384]{2,0,1:T(4,128)(2,1)}, bf16[32,1536]{1,0:T(8,128)(2,1)}), (bf16[4,1536,384]{2,0,1:T(4,128)(2,1)}, bf16[32,1536]{1,0:T(8,128)(2,1)})) %all-reduce.8.cloned.1.call-update) | async-done | bytes 4816912
  (282 shorter events, 74.7 us)
Async XLA Ops:
  7.2 62.9 %all-gather.5.cloned.1.call-start = ((), (), s32[]{:S(2)}) async-start(), calls=%async_computation.2 | async-start | bytes 2654208 | tf_op jit(solution)/shard_map/all_gather | solution.py:165
  10.5 118.0 %all-gather.3.cloned.1.call-start = ((), (), s32[]{:S(2)}) async-start(), calls=%async_computation.1 | async-start | bytes 2654208 | tf_op jit(solution)/shard_map/all_gather | solution.py:166
  13.3 209.8 %all-reduce.6.cloned.1.call-start = ((), (), s32[]{:S(2)}) async-start(), calls=%async_computation.3 | async-start | bytes 2359296 | tf_op jit(solution)/shard_map/psum | solution.py:172
  162.3 9.5 %slice-start.4 = ((s8[5898240]{0:T(1024)(128)(4,1)}), s8[4194304]{0:T(1024)(128)(4,1)S(1)}, s32[]{:S(2)}) async-start(s8[5898240]{0:T(1024)(128)(4,1)} %bitcast.122), calls=%async_computation.10 | async-start | bytes 8388608
  178.0 46.7 %copy-start.3 = (bf16[1,384,1536]{2,1,0:T(8,128)(2,1)S(1)}, bf16[1,384,1536]{2,1,0:T(8,128)(2,1)}, u32[]{:S(2)}) copy-start(bf16[1,384,1536]{2,1,0:T(8,128)(2,1)} %param.9) | copy-start | bytes 3538948
  178.0 276.5 %reduce-scatter.2.cloned.1.call-start = ((), (), s32[]{:S(2)}) async-start(), calls=%async_computation.4 | async-start | bytes 5308416 | tf_op jit(solution)/shard_map/reduce_scatter | solution.py:195
  223.1 13.3 %copy-start.4 = (bf16[1,384,1536]{2,1,0:T(8,128)(2,1)S(1)}, bf16[1,384,1536]{2,1,0:T(8,128)(2,1)}, u32[]{:S(2)}) copy-start(bf16[1,384,1536]{2,1,0:T(8,128)(2,1)} %param.9) | copy-start | bytes 3538948
  224.7 13.3 %copy-start.6 = (bf16[384,1536]{1,0:T(8,128)(2,1)}, bf16[384,1536]{1,0:T(8,128)(2,1)S(1)}, u32[]{:S(2)}) copy-start(bf16[384,1536]{1,0:T(8,128)(2,1)S(1)} %add_convert_fusion.1) | copy-start | bytes 3538948
  224.7 6.6 %collective-permute-start = (bf16[16,3072]{1,0:T(8,128)(2,1)S(1)}, bf16[16,3072]{1,0:T(8,128)(2,1)S(1)}, u32[]{:S(2)}, u32[]{:S(2)}) collective-permute-start(bf16[16,3072]{1,0:T(8,128)(2,1)S(1)} %get-tuple-element.83), channel_id=1, source_target_pairs={{0,4},{4,8},{8,12},{12,16},{16,20},{20,24},{24,28},{1,5},{5,9},{9,... | collective-permute-start | bytes 294920 | tf_op jit(solution)/shard_map/ppermute | solution.py:18
  229.5 6.9 %collective-permute-start.1 = (bf16[16,3072]{1,0:T(8,128)(2,1)S(1)}, bf16[16,3072]{1,0:T(8,128)(2,1)S(1)}, u32[]{:S(2)}, u32[]{:S(2)}) collective-permute-start(bf16[16,3072]{1,0:T(8,128)(2,1)S(1)} %get-tuple-element.84), channel_id=1, source_target_pairs={{4,0},{8,4},{12,8},{16,12},{20,16},{24,20},{28,24},{5,1},{9,5},{13... | collective-permute-start | bytes 294920 | tf_op jit(solution)/shard_map/ppermute | solution.py:19
  231.1 7.0 %copy-start.55 = (f32[1536]{0:T(1024)}, f32[1536]{0:T(1024)S(1)}, u32[]{:S(2)}) copy-start(f32[1536]{0:T(1024)S(1)} %get-tuple-element.66) | copy-start | bytes 18436
  231.1 7.0 %copy-start.57 = (f32[1536]{0:T(1024)}, f32[1536]{0:T(1024)S(1)}, u32[]{:S(2)}) copy-start(f32[1536]{0:T(1024)S(1)} %get-tuple-element.67) | copy-start | bytes 18436
  231.1 7.0 %copy-start.59 = (f32[1536]{0:T(1024)}, f32[1536]{0:T(1024)S(1)}, u32[]{:S(2)}) copy-start(f32[1536]{0:T(1024)S(1)} %get-tuple-element.68) | copy-start | bytes 18436
  231.1 7.0 %copy-start.61 = (f32[1536]{0:T(1024)}, f32[1536]{0:T(1024)S(1)}, u32[]{:S(2)}) copy-start(f32[1536]{0:T(1024)S(1)} %get-tuple-element.69) | copy-start | bytes 18436
  231.1 7.0 %copy-start.63 = (f32[1536]{0:T(1024)}, f32[1536]{0:T(1024)S(1)}, u32[]{:S(2)}) copy-start(f32[1536]{0:T(1024)S(1)} %get-tuple-element.70) | copy-start | bytes 18436
  231.1 7.0 %copy-start.65 = (f32[1536]{0:T(1024)}, f32[1536]{0:T(1024)S(1)}, u32[]{:S(2)}) copy-start(f32[1536]{0:T(1024)S(1)} %get-tuple-element.71) | copy-start | bytes 18436
  231.1 7.0 %copy-start.67 = (f32[1536]{0:T(1024)}, f32[1536]{0:T(1024)S(1)}, u32[]{:S(2)}) copy-start(f32[1536]{0:T(1024)S(1)} %get-tuple-element.72) | copy-start | bytes 18436
  231.1 7.0 %copy-start.69 = (f32[1536]{0:T(1024)}, f32[1536]{0:T(1024)S(1)}, u32[]{:S(2)}) copy-start(f32[1536]{0:T(1024)S(1)} %get-tuple-element.73) | copy-start | bytes 18436
  238.0 10.3 %copy-start = (bf16[400,3072]{1,0:T(8,128)(2,1)}, bf16[400,3072]{1,0:T(8,128)(2,1)S(1)}, u32[]{:S(2)}) copy-start(bf16[400,3072]{1,0:T(8,128)(2,1)S(1)} %get-tuple-element.82) | copy-start | bytes 7372804
  253.3 8.5 %slice-start = ((s8[6291456]{0:T(1024)(128)(4,1)}), s8[4194304]{0:T(1024)(128)(4,1)S(1)}, s32[]{:S(2)}) async-start(s8[6291456]{0:T(1024)(128)(4,1)} %bitcast.113), calls=%async_computation.6 | async-start | bytes 8388608
  253.4 8.1 %copy-start.17 = (bf16[6,4,96,64]{2,3,1,0:T(8,128)(2,1)S(1)}, bf16[6,4,96,64]{2,3,1,0:T(8,128)(2,1)}, u32[]{:S(2)}) copy-start(bf16[6,4,96,64]{2,3,1,0:T(8,128)(2,1)} %copy-done.16) | copy-start | bytes 884740
  253.4 8.4 %slice-start.1 = ((s8[6291456]{0:T(1024)(128)(4,1)}), s8[2097152]{0:T(1024)(128)(4,1)S(1)}, s32[]{:S(2)}) async-start(s8[6291456]{0:T(1024)(128)(4,1)} %bitcast.113), calls=%async_computation.7 | async-start | bytes 4194304
  253.4 8.4 %copy-start.82 = (f32[3,8,64]{2,1,0:T(8,128)S(1)}, f32[3,8,64]{2,1,0:T(8,128)}, u32[]{:S(2)}) copy-start(f32[3,8,64]{2,1,0:T(8,128)} %copy-done.81) | copy-start | bytes 18436
  280.7 15.5 %copy-start.84 = (s32[90]{0:T(128)S(1)}, s32[90]{0:T(128)}, u32[]{:S(2)}) copy-start(s32[90]{0:T(128)} %min.18) | copy-start | bytes 1084
  280.7 15.5 %copy-start.85 = (pred[90]{0:T(512)(128)(4,1)S(1)}, pred[90]{0:T(512)(128)(4,1)}, u32[]{:S(2)}) copy-start(pred[90]{0:T(512)(128)(4,1)} %and.19) | copy-start | bytes 274
  364.2 218.6 %all-reduce.8.cloned.1.call-start = ((), (), s32[]{:S(2)}) async-start(), calls=%async_computation.5 | async-start | bytes 9633792
  366.1 15.4 %copy-start.1 = (bf16[400,3072]{1,0:T(8,128)(2,1)S(1)}, bf16[400,3072]{1,0:T(8,128)(2,1)}, u32[]{:S(2)}) copy-start(bf16[400,3072]{1,0:T(8,128)(2,1)} %copy-done) | copy-start | bytes 7372804
  366.1 15.4 %copy-start.5 = (bf16[1,384,1536]{2,1,0:T(8,128)(2,1)S(1)}, bf16[1,384,1536]{2,1,0:T(8,128)(2,1)}, u32[]{:S(2)}) copy-start(bf16[1,384,1536]{2,1,0:T(8,128)(2,1)} %param.9) | copy-start | bytes 3538948
  366.1 15.4 %copy-start.7 = (bf16[384,1536]{1,0:T(8,128)(2,1)S(1)}, bf16[384,1536]{1,0:T(8,128)(2,1)}, u32[]{:S(2)}) copy-start(bf16[384,1536]{1,0:T(8,128)(2,1)} %copy-done.6) | copy-start | bytes 3538948
  366.1 30.1 %slice-start.2 = ((s8[5898240]{0:T(1024)(128)(4,1)}), s8[4194304]{0:T(1024)(128)(4,1)S(1)}, s32[]{:S(2)}) async-start(s8[5898240]{0:T(1024)(128)(4,1)} %bitcast.118), calls=%async_computation.8 | async-start | bytes 8388608
  381.5 14.7 %slice-start.3 = ((s8[5898240]{0:T(1024)(128)(4,1)}), s8[1703936]{0:T(1024)(128)(4,1)S(1)}, s32[]{:S(2)}) async-start(s8[5898240]{0:T(1024)(128)(4,1)} %bitcast.118), calls=%async_computation.9 | async-start | bytes 3407872
  381.5 14.7 %copy-start.12 = (bf16[6,4,64,960]{3,2,1,0:T(8,128)(2,1)S(1)}, bf16[6,4,64,960]{3,2,1,0:T(8,128)(2,1)}, u32[]{:S(2)}) copy-start(bf16[6,4,64,960]{3,2,1,0:T(8,128)(2,1)} %multiply_convert_fusion) | copy-start | bytes 8847364
  (68 other events, 228.7 us)
Sparse Core Ops, SparseCore 0:
  10.9 59.1 all-gather.4
  72.9 55.4 all-gather.2
  178.1 44.8 all-reduce.5
  364.3 90.1 reduce-scatter.1
  470.0 112.7 all-reduce.7
where the time goes:
time: 605 us; the launch traced here: 593 us
  waiting for transfers between devices  286 us (47%)
  local copies, waits for them, and re-layouts  158 us (26%)
  matrix products  68.2 us (11%)
  other arithmetic  58.4 us (10%)
  between operations  16.1 us (3%)
  starting transfers between devices  6.28 us (1%)
    unnamed x6, waiting for transfers between devices  92.3 us
    all_gather x1, waiting for transfers between devices, shards(): lax.all_gather(key_rows, 'tm', axis=0, tiled=True)  53.7 us
    all_gather x1, waiting for transfers between devices, shards(): lax.all_gather(values, 'tm', axis=0, tiled=True)  47.1 us
    reduce_scatter x1, waiting for transfers between devices, shards(): lax.psum_scatter(key_value_terms.astype(jnp.bfloat16), 'tm', scatter_dime...  45.4 us
    psum x1, waiting for transfers between devices, shards(): lax.psum(output_part.astype(jnp.bfloat16), 'head').astype(jnp.float32)  42.8 us
    gather x4, local copies, waits for them, and re-layouts, gather_blocks(): gathered = source.reshape(-1, block_len, head_count, head_dim)[listed]  26.8 us
    another operation x33, local copies, waits for them, and re-layouts, conv_apply(): jnp.stack(taps_grad)  24.5 us
    reshape x4, local copies, waits for them, and re-layouts, gather_blocks(): gathered = source.reshape(-1, block_len, head_count, head_dim)[listed]  22.6 us
  transfers between devices with their start and end apart: 7, of which 6 were waited for; matrix products, arithmetic and copies ran while one was open for 14% of the time, Pallas kernels for 0%

commit v1 on v0

v1 whole, which is shorter than its diff:
```python
import jax
import jax.numpy as jnp
from jax import lax
from jax.experimental import pallas as pl
from jax.experimental.pallas import tpu as pltpu
from jax.sharding import PartitionSpec as P

HD = 96
BLK = 64
KW = 32
HALF = KW // 2
T = 384
C = 1536
F = 384
NKB = 48
QC = 256
MESH = pl.DeviceIdType.MESH
BF = jnp.bfloat16
F32 = jnp.float32


def remote(src, dst, ssem, rsem, device):
    return pltpu.make_async_remote_copy(
        src_ref=src, dst_ref=dst, send_sem=ssem, recv_sem=rsem, device_id=device, device_id_type=MESH
    )


def greet(devices):
    barrier = pltpu.get_barrier_semaphore()
    for device in devices:
        pl.semaphore_signal(barrier, inc=1, device_id=device, device_id_type=MESH)
    pl.semaphore_wait(barrier, len(devices))


def place():
    dp, tm, hd = lax.axis_index("dp"), lax.axis_index("tm"), lax.axis_index("head")
    return dp, tm, hd


def tap_terms(window, offsets):
    for r in range(8):
        shifted = window[r : r + 88] if r else window
        for a in range(5):
            o = 8 * a + r
            if o in offsets:
                yield offsets[o], shifted[8 * a : 8 * a + 64]


def project_kernel(
    frames, cot, w, taps, meta, kv_out, qd_out, bg_t, frames_t,
    bg, upad, halo, tapsf, kv_s, q_s, d_s, hs, hr, kvs, kvr, qs, qr, ds, dr, ls,
):
    dp, tm, hd = place()
    x, zh = tm // 2, lax.rem(tm, 2)
    at_tm = lambda k: (dp, lax.rem(tm + k, 8), hd)
    greet([at_tm(k) for k in range(1, 8)])
    halos = [
        remote(cot.at[T - HALF : T], halo.at[0], hs.at[0], hr.at[0], at_tm(1)),
        remote(cot.at[0:HALF], halo.at[1], hs.at[1], hr.at[1], at_tm(7)),
    ]
    for c in halos:
        c.start()

    for p in (1, 2):
        y = jnp.dot(frames[...], w[p], preferred_element_type=F32).astype(BF).T
        for h in range(4):
            kv_s[h, (p - 1) * HD : p * HD, :] = y[h * HD : (h + 1) * HD]
    sends = []
    for k in range(1, 8):
        c = remote(kv_s.at[lax.rem(tm + k, 8) // 2], kv_out.at[tm], kvs.at[k], kvr.at[k], at_tm(k))
        c.start()
        sends.append(c)
    local = [pltpu.make_async_copy(kv_s.at[x], kv_out.at[tm], ls.at[0])]
    local[0].start()

    y = jnp.dot(frames[...], w[0], preferred_element_type=F32).astype(BF).T
    for h in range(4):
        q_s[h] = y[h * HD : (h + 1) * HD]
    for k in range(1, 4):
        xo = lax.rem(x + k, 4)
        c = remote(q_s.at[xo], qd_out.at[x, 0:HD], qs.at[k], qr.at[k], (dp, xo * 2 + zh, hd))
        c.start()
        sends.append(c)
    c = pltpu.make_async_copy(q_s.at[x], qd_out.at[x, 0:HD], ls.at[1])
    c.start()
    local.append(c)

    tapsf[...] = taps[...].astype(F32)
    upad[HALF : HALF + T] = cot[...].astype(F32)
    for c in halos:
        c.wait()
    upad[0:HALF] = jnp.where(tm > 0, halo[0].astype(F32), 0.0)
    upad[HALF + T :] = jnp.where(tm < 7, halo[1].astype(F32), 0.0)
    offsets = {2 * HALF - j: j for j in range(KW)}

    def conv(it, carry):
        i, l = it // 12, lax.rem(it, 12)
        lanes = pl.ds(pl.multiple_of(l * 128, 128), 128)
        window = upad[pl.ds(pl.multiple_of(i * 64, 64), 96), lanes]
        acc = window[HALF : HALF + 64]
        for j, rows in tap_terms(window, offsets):
            acc = acc + tapsf[j : j + 1, lanes] * rows
        bg[pl.ds(pl.multiple_of(i * 64, 64), 64), lanes] = acc.astype(BF)
        return carry

    lax.fori_loop(0, 72, conv, 0)
    y = jnp.dot(bg[...], w[3], preferred_element_type=F32).astype(BF).T
    for h in range(4):
        d_s[h, 0:HD] = y[h * HD : (h + 1) * HD]
        d_s[h, HD:] = meta[...]
    for k in range(1, 4):
        xo = lax.rem(x + k, 4)
        c = remote(d_s.at[xo], qd_out.at[x, HD:], ds.at[k], dr.at[k], (dp, xo * 2 + zh, hd))
        c.start()
        sends.append(c)
    c = pltpu.make_async_copy(d_s.at[x], qd_out.at[x, HD:], ls.at[2])
    c.start()
    local.append(c)

    frames_t[...] = frames[...].T
    bg_t[...] = bg[...].T
    for c in local:
        c.wait()
    for c in sends:
        c.wait()


def project(frames, cot, w, taps, meta):
    vmem = pl.BlockSpec(memory_space=pltpu.VMEM)
    anym = pl.BlockSpec(memory_space=pl.ANY)
    dma = pltpu.SemaphoreType.DMA
    return pl.pallas_call(
        project_kernel,
        out_shape=(
            jax.ShapeDtypeStruct((8, 2 * HD, T), BF),
            jax.ShapeDtypeStruct((4, 2 * HD + 16, T), BF),
            jax.ShapeDtypeStruct((C, T), BF),
            jax.ShapeDtypeStruct((C, T), BF),
        ),
        in_specs=[vmem] * 5,
        out_specs=(anym, anym, vmem, vmem),
        scratch_shapes=[
            pltpu.VMEM((T, C), BF),
            pltpu.VMEM((T + 2 * HALF, C), F32),
            pltpu.VMEM((2, HALF, C), BF),
            pltpu.VMEM((KW, C), F32),
            pltpu.VMEM((4, 2 * HD, T), BF),
            pltpu.VMEM((4, HD, T), BF),
            pltpu.VMEM((4, HD + 16, T), BF),
            dma((2,)), dma((2,)), dma((8,)), dma((8,)), dma((4,)), dma((4,)), dma((4,)), dma((4,)), dma((3,)),
        ],
        compiler_params=pltpu.CompilerParams(
            collective_id=0, has_side_effects=True, vmem_limit_bytes=48 << 20
        ),
        name="project_exchange",
    )(frames, cot, w, taps, meta)


def attention_kernel(
    kv, qd, qblock, o_out, dq_out, dkv_out,
    kn, vn, kt, vt, qt, dt, on, dqn, live, dk, dv, st, et,
):
    scale = HD ** -0.5
    c2 = scale * 1.4426950408889634
    for t in range(8):
        kt[:, t * T : (t + 1) * T] = kv[t, 0:HD]
        vt[:, t * T : (t + 1) * T] = kv[t, HD:]
        kn[t * T : (t + 1) * T, :] = kv[t, 0:HD].T
        vn[t * T : (t + 1) * T, :] = kv[t, HD:].T
    for a in range(4):
        lanes = slice(a * T, (a + 1) * T)
        qt[:, lanes] = qd[a, 0:HD]
        dt[:, lanes] = qd[a, HD : 2 * HD]
        meta = qd[a, 2 * HD :].astype(F32)
        phase, count = meta[0:1], meta[1:2]
        row = lax.broadcasted_iota(jnp.int32, (64, T), 0)
        kb = (row // 8) * 6 + lax.rem(row, 8)
        far = (lax.rem(kb, 4).astype(F32) == phase) & ((kb // 4).astype(F32) < count)
        near = jnp.abs(kb.astype(F32) - qblock[a : a + 1]) < 1.5
        live[:, lanes] = jnp.where(far | near, 1.0, 0.0)
    dk[...] = jnp.zeros_like(dk)
    dv[...] = jnp.zeros_like(dv)

    def step(c, carry):
        lanes = pl.ds(pl.multiple_of(c * QC, QC), QC)
        q_t = qt[:, lanes]

        def scores(t, top):
            rows = pl.ds(pl.multiple_of(t * T, T), T)
            s = jnp.dot(kn[rows, :], q_t, preferred_element_type=F32)
            mask = live[pl.ds(pl.multiple_of(t * 8, 8), 8), lanes]
            parts = []
            for b in range(6):
                part = jnp.where(mask[b : b + 1] > 0.5, s[b * BLK : (b + 1) * BLK], -1e30)
                top = jnp.maximum(top, jnp.max(part.reshape(8, 8, QC), axis=0))
                parts.append(part)
            st[rows, :] = jnp.concatenate(parts, axis=0)
            return top

        top = lax.fori_loop(0, 8, scores, jnp.full((8, QC), -jnp.inf, F32))
        top = jnp.max(top, axis=0, keepdims=True) * c2

        def weigh(t, carry):
            total, o = carry
            rows = pl.ds(pl.multiple_of(t * T, T), T)
            e = jnp.exp2(st[rows, :] * c2 - top)
            total = total + jnp.sum(e.reshape(T // 8, 8, QC), axis=0)
            eb = e.astype(BF)
            et[rows, :] = eb
            o = o + jnp.dot(vt[:, pl.ds(pl.multiple_of(t * T, T), T)], eb, preferred_element_type=F32)
            return total, o

        total, o = lax.fori_loop(
            0, 8, weigh, (jnp.zeros((8, QC), F32), jnp.zeros((HD, QC), F32))
        )
        inverse = 1.0 / jnp.sum(total, axis=0, keepdims=True)
        o = (o * inverse).astype(BF)
        on[:, lanes] = o
        d = dt[:, lanes].astype(F32)
        delta = jnp.sum(d * o.astype(F32), axis=0, keepdims=True) * inverse
        d_t = (d * inverse).astype(BF)
        d_n = d_t.T
        q_n = q_t.T

        def back(t, dq):
            rows = pl.ds(pl.multiple_of(t * T, T), T)
            eb = et[rows, :]
            dp = jnp.dot(vn[rows, :], d_t, preferred_element_type=F32)
            ds = (eb.astype(F32) * (dp - delta)).astype(BF)
            dk[rows, :] += jnp.dot(ds, q_n, preferred_element_type=F32)
            dv[rows, :] += jnp.dot(eb, d_n, preferred_element_type=F32)
            return dq + jnp.dot(
                kt[:, pl.ds(pl.multiple_of(t * T, T), T)], ds, preferred_element_type=F32
            )

        dq = lax.fori_loop(0, 8, back, jnp.zeros((HD, QC), F32))
        dqn[:, lanes] = (dq * scale).astype(BF)
        return carry

    lax.fori_loop(0, 4 * T // QC, step, 0)
    for a in range(4):
        lanes = slice(a * T, (a + 1) * T)
        o_out[a] = on[:, lanes]
        dq_out[a] = dqn[:, lanes]
    for t in range(8):
        dkv_out[t, 0:HD] = (dk[t * T : (t + 1) * T, :] * scale).astype(BF).T
        dkv_out[t, HD:] = dv[t * T : (t + 1) * T, :].astype(BF).T


def attention(kv, qd, qblock):
    vmem = pl.BlockSpec(memory_space=pltpu.VMEM)
    keys, queries = 8 * T, 4 * T
    return pl.pallas_call(
        attention_kernel,
        out_shape=(
            jax.ShapeDtypeStruct((4, HD, T), BF),
            jax.ShapeDtypeStruct((4, HD, T), BF),
            jax.ShapeDtypeStruct((8, 2 * HD, T), BF),
        ),
        in_specs=[vmem] * 3,
        out_specs=(vmem, vmem, vmem),
        scratch_shapes=[
            pltpu.VMEM((keys, HD), BF), pltpu.VMEM((keys, HD), BF),
            pltpu.VMEM((HD, keys), BF), pltpu.VMEM((HD, keys), BF),
            pltpu.VMEM((HD, queries), BF), pltpu.VMEM((HD, queries), BF),
            pltpu.VMEM((HD, queries), BF), pltpu.VMEM((HD, queries), BF),
            pltpu.VMEM((64, queries), F32),
            pltpu.VMEM((keys, HD), F32), pltpu.VMEM((keys, HD), F32),
            pltpu.VMEM((keys, QC), F32), pltpu.VMEM((keys, QC), BF),
        ],
        compiler_params=pltpu.CompilerParams(vmem_limit_bytes=48 << 20),
        name="attention_both",
    )(kv, qd, qblock)


def finish_kernel(
    frames, cot, w3, taps, bg_t, frames_t, o_in, dq_in, dkv_in,
    enc_out, pg_out, kg_out,
    mix_r, dq_r, dkv_r, op_s, op_r, g_s, g_r, h1, s1_r, h2, s2_r, rpad, res, halo, tapsf, enc, kacc, kg, kr, kgy,
    a_s, a_r, b_s, b_r, c_s, c_r, ls, os_, or_, gs, gr, s1s, s1r, s2s, s2r, hs, hr, es, er, ks, kr_s, ys, yr,
):
    dp, tm, hd = place()
    zl, core = dp // 2, lax.rem(dp, 2)
    x, zh = tm // 2, lax.rem(tm, 2)
    z = zh * 2 + zl
    at_tm = lambda k: (dp, lax.rem(tm + k, 8), hd)
    at_x = lambda k: (dp, lax.rem(x + k, 4) * 2 + zh, hd)
    at_y = lambda k: (dp, tm, lax.rem(hd + k, 4))

    def at_z(k):
        to = lax.rem(z + k, 4)
        return (lax.rem(to, 2) * 2 + core, x * 2 + to // 2, hd)

    me = dp * 8 + tm

    def at_plane(k):
        to = lax.rem(me + k, 32)
        return (to // 8, lax.rem(to, 8), hd)

    partner = (zl * 2 + 1 - core, tm, hd)
    greet([at_plane(k) for k in range(1, 32)] + [at_y(k) for k in range(1, 4)])

    waits = []

    def go(c):
        c.start()
        return c

    mix_c, dq_c, dkv_c = [], [], []
    for k in range(1, 4):
        xo = lax.rem(x + k, 4)
        mix_c.append(go(remote(o_in.at[xo], mix_r.at[x], a_s.at[k], a_r.at[k], at_x(k))))
    mix_c.append(go(pltpu.make_async_copy(o_in.at[x], mix_r.at[x], ls.at[0])))
    for k in range(1, 4):
        xo = lax.rem(x + k, 4)
        dq_c.append(go(remote(dq_in.at[xo], dq_r.at[x], b_s.at[k], b_r.at[k], at_x(k))))
    dq_c.append(go(pltpu.make_async_copy(dq_in.at[x], dq_r.at[x], ls.at[1])))
    for k in range(1, 8):
        to = lax.rem(tm + k, 8)
        dkv_c.append(go(remote(dkv_in.at[to], dkv_r.at[zh, x], c_s.at[k], c_r.at[k], at_tm(k))))
    dkv_c.append(go(pltpu.make_async_copy(dkv_in.at[tm], dkv_r.at[zh, x], ls.at[2])))

    tapsf[...] = taps[:, pl.ds(pl.multiple_of(hd * F, 128), F)].astype(F32)
    kacc[...] = jnp.zeros_like(kacc)

    for c in mix_c:
        c.wait()
    mixed = mix_r[...].reshape(F, T).T
    nt = (((1,), (1,)), ((), ()))
    op_c = []
    for k in range(1, 4):
        rows = pl.ds(pl.multiple_of(lax.rem(hd + k, 4) * F, F), F)
        op_s[k] = lax.dot_general(mixed, w3[rows, :], nt, preferred_element_type=F32).astype(BF)
        op_c.append(go(remote(op_s.at[k], op_r.at[k], os_.at[k], or_.at[k], at_y(k))))

    def away(p, left, right):
        for l in range(2):
            rows = pl.ds(pl.multiple_of((l * 2 + 1 - core) * F, F), F)
            g_s[p, l] = jnp.dot(left[rows, :], right, preferred_element_type=F32).astype(BF)
        return go(remote(g_s.at[p], g_r.at[p], gs.at[p], gr.at[p], partner))

    def keep(p, left, right, copy, by_x):
        copy.wait()
        for l in range(2):
            rows = pl.ds(pl.multiple_of((l * 2 + core) * F, F), F)
            g = jnp.dot(left[rows, :], right, preferred_element_type=F32) + g_r[p, l].astype(F32)
            g = g.astype(BF)
            for xo in range(4):
                for h in range(2):
                    piece = g[xo * 96 + h * 48 : xo * 96 + h * 48 + 48]
                    if by_x:
                        h1[p, xo * 4 + h * 2 + l] = piece
                    else:
                        h1[p, (h * 2 + l) * 4 + xo] = piece
        out = []
        for k in range(1, 4):
            to = lax.rem((x if by_x else z) + k, 4)
            device = at_x(k) if by_x else at_z(k)
            out.append(
                go(remote(h1.at[p, pl.ds(to * 4, 4)], s1_r.at[p, k], s1s.at[p, k], s1r.at[p, k], device))
            )
        return out

    def second(p, copies, by_x):
        for c in copies:
            c.wait()
        own = h1[p, pl.ds((x if by_x else z) * 4, 4)].astype(F32)
        for k in range(1, 4):
            own = own + s1_r[p, k].astype(F32)
        h2[p] = own.astype(BF)
        out = []
        for k in range(1, 4):
            to = lax.rem((z if by_x else x) + k, 4)
            device = at_z(k) if by_x else at_x(k)
            out.append(go(remote(h2.at[p, to], s2_r.at[p, k], s2s.at[p, k], s2r.at[p, k], device)))
        return out

    def last(p, copies, by_x):
        for c in copies:
            c.wait()
        own = h2[p, z if by_x else x].astype(F32)
        for k in range(1, 4):
            own = own + s2_r[p, k].astype(F32)
        pg_out[p] = own

    g3 = away(3, bg_t, mixed)
    for c in dq_c:
        c.wait()
    dq = dq_r[...].reshape(F, T).T
    g0 = away(0, frames_t, dq)
    r3 = keep(3, bg_t, mixed, g3, True)
    r0 = keep(0, frames_t, dq, g0, False)

    rows = pl.ds(pl.multiple_of(hd * F, F), F)
    summed = lax.dot_general(mixed, w3[rows, :], nt, preferred_element_type=F32)
    for c in op_c:
        c.wait()
    for k in range(1, 4):
        summed = summed + op_r[k].astype(F32)
    lanes = pl.ds(pl.multiple_of(hd * F, 128), F)
    res[...] = (frames[:, lanes].astype(F32) + summed).astype(BF)
    halos = [
        go(remote(res.at[T - HALF : T], halo.at[0], hs.at[0], hr.at[0], at_tm(1))),
        go(remote(res.at[0:HALF], halo.at[1], hs.at[1], hr.at[1], at_tm(7))),
    ]

    for c in dkv_c:
        c.wait()
    both = (dkv_r[0].astype(F32) + dkv_r[1].astype(F32)).astype(BF)
    dk = both[:, 0:HD].reshape(F, T).T
    dv = both[:, HD:].reshape(F, T).T
    g1 = away(1, frames_t, dk)
    g2 = away(2, frames_t, dv)
    r1 = keep(1, frames_t, dk, g1, True)
    r2 = keep(2, frames_t, dv, g2, False)

    rpad[HALF : HALF + T] = res[...].astype(F32)
    for c in halos:
        c.wait()
    rpad[0:HALF] = jnp.where(tm > 0, halo[0].astype(F32), 0.0)
    rpad[HALF + T :] = jnp.where(tm < 7, halo[1].astype(F32), 0.0)
    offsets = {j: j for j in range(KW)}

    def conv(it, carry):
        i, l = it // 3, lax.rem(it, 3)
        lane = pl.ds(pl.multiple_of(l * 128, 128), 128)
        window = rpad[pl.ds(pl.multiple_of(i * 64, 64), 96), lane]
        up = cot[
            pl.ds(pl.multiple_of(i * 64, 64), 64), pl.ds(pl.multiple_of(hd * F + l * 128, 128), 128)
        ].astype(F32)
        acc = window[HALF : HALF + 64]
        for j, rows in tap_terms(window, offsets):
            acc = acc + tapsf[j : j + 1, lane] * rows
            kacc[j, :, lane] += jnp.sum((up * rows).reshape(8, 8, 128), axis=0)
        enc[pl.ds(pl.multiple_of(i * 64, 64), 64), lane] = acc.astype(BF)
        return carry

    lax.fori_loop(0, 18, conv, 0)
    enc_c = [go(pltpu.make_async_copy(enc, enc_out.at[:, lanes], ls.at[3]))]
    for k in range(1, 4):
        enc_c.append(go(remote(enc, enc_out.at[:, lanes], es.at[k], er.at[k], at_y(k))))
    for j in range(KW):
        kg[j] = jnp.sum(kacc[j], axis=0, keepdims=True)
    kg_c = []
    for k in range(1, 32):
        to = lax.rem(me + k, 32)
        kg_c.append(go(remote(kg.at[to], kr.at[k], ks.at[k], kr_s.at[k], at_plane(k))))

    t3 = second(3, r3, True)
    t0 = second(0, r0, False)
    t1 = second(1, r1, True)
    t2 = second(2, r2, False)
    for c in kg_c:
        c.wait()
    total = kg[me]
    for k in range(1, 32):
        total = total + kr[k]
    kgy[hd] = total
    ky_c = [go(remote(kgy.at[hd], kgy.at[hd], ys.at[k], yr.at[k], at_y(k))) for k in range(1, 4)]
    last(3, t3, True)
    last(0, t0, False)
    last(1, t1, True)
    last(2, t2, False)
    for c in ky_c:
        c.wait()
    for y in range(4):
        kg_out[:, y * F : (y + 1) * F] = kgy[y]
    for c in enc_c:
        c.wait()


def finish(frames, cot, w3, taps, bg_t, frames_t, o, dq, dkv):
    vmem = pl.BlockSpec(memory_space=pltpu.VMEM)
    anym = pl.BlockSpec(memory_space=pl.ANY)
    dma = pltpu.SemaphoreType.DMA
    return pl.pallas_call(
        finish_kernel,
        out_shape=(
            jax.ShapeDtypeStruct((T, C), BF),
            jax.ShapeDtypeStruct((4, 48, F), F32),
            jax.ShapeDtypeStruct((1, C), F32),
        ),
        in_specs=[vmem] * 6 + [anym] * 3,
        out_specs=(anym, vmem, vmem),
        scratch_shapes=[
            pltpu.VMEM((4, HD, T), BF),
            pltpu.VMEM((4, HD, T), BF),
            pltpu.VMEM((2, 4, 2 * HD, T), BF),
            pltpu.VMEM((4, T, F), BF),
            pltpu.VMEM((4, T, F), BF),
            pltpu.VMEM((4, 2, F, F), BF),
            pltpu.VMEM((4, 2, F, F), BF),
            pltpu.VMEM((4, 16, 48, F), BF),
            pltpu.VMEM((4, 4, 4, 48, F), BF),
            pltpu.VMEM((4, 4, 48, F), BF),
            pltpu.VMEM((4, 4, 48, F), BF),
            pltpu.VMEM((T + 2 * HALF, F), F32),
            pltpu.VMEM((T, F), BF),
            pltpu.VMEM((2, HALF, F), BF),
            pltpu.VMEM((KW, F), F32),
            pltpu.VMEM((T, F), BF),
            pltpu.VMEM((KW, 8, F), F32),
            pltpu.VMEM((KW, 1, F), F32),
            pltpu.VMEM((KW, 1, F), F32),
            pltpu.VMEM((4, 1, F), F32),
            dma((4,)), dma((4,)), dma((4,)), dma((4,)), dma((8,)), dma((8,)), dma((4,)),
            dma((4,)), dma((4,)), dma((4,)), dma((4,)), dma((4, 4)), dma((4, 4)), dma((4, 4)), dma((4, 4)),
            dma((2,)), dma((2,)), dma((4,)), dma((4,)), dma((32,)), dma((32,)), dma((4,)), dma((4,)),
        ],
        compiler_params=pltpu.CompilerParams(
            collective_id=1, has_side_effects=True, vmem_limit_bytes=48 << 20
        ),
        name="finish_exchange",
    )(frames, cot, w3, taps, bg_t, frames_t, o, dq, dkv)


def shards(frames, projections, kernel, pattern, cotangent):
    source, upstream, rows_pattern = frames[0], cotangent[0], pattern[0]
    phase = jnp.repeat(rows_pattern[:, 0], BLK).astype(BF)
    count = jnp.repeat(jnp.sum((rows_pattern >= 0).astype(jnp.int32), axis=1), BLK).astype(BF)
    row = lax.broadcasted_iota(jnp.int32, (16, T), 0)
    meta = jnp.where(row == 0, phase[None], jnp.where(row == 1, count[None], jnp.zeros((), BF)))
    zh = lax.rem(lax.axis_index("tm"), 2)
    owner = jnp.arange(4)[:, None] * 2 + zh
    qblock = (owner * (T // BLK) + jnp.arange(T)[None, :] // BLK).astype(F32)
    kv, qd, bg_t, frames_t = project(source, upstream, projections, kernel, meta)
    o, dq, dkv = attention(kv, qd, qblock)
    enc, pg, kg = finish(source, upstream, projections[3], kernel, bg_t, frames_t, o, dq, dkv)
    return enc[None], pg, kg


def solution(mesh):
    placed = (
        P("dp", "tm", None),
        P(None, None, "head"),
        P(),
        P("dp", "tm", None),
        P("dp", "tm", None),
    )
    return jax.shard_map(
        shards,
        mesh=mesh,
        in_specs=placed,
        out_specs=(P("dp", "tm", None), P(None, ("dp", "tm"), "head"), P(("dp", "tm"), None)),
        check_vma=False,
    )
```

time: 605 us -> 155 us (0.26); the launches traced: 593 us -> 153 us
  waiting for transfers between devices: 286 us -> 0 us
  local copies, waits for them, and re-layouts: 158 us -> 9.93 us
  Pallas kernels: 0 us -> 140 us
  matrix products: 68.2 us -> 0 us
  other arithmetic: 58.4 us -> 1.75 us
  between operations: 16.1 us -> 0.72 us
  starting transfers between devices: 6.28 us -> 0 us
    pallas_call x0 -> x3, Pallas kernels: none -> 140 us  [the longest x1 66.9 us: finish(): pl.pallas_call(finish_kernel, out_shape=(jax.ShapeDtypeStruct((T, C), BF)...]
    all_gather x2 -> x0, waiting for transfers between devices: 101 us -> none  [the longest x1 53.7 us: shards(): lax.all_gather(key_rows, 'tm', axis=0, tiled=True)]
    unnamed x6 -> x0, waiting for transfers between devices: 92.3 us -> none
    dot_general x17 -> x0, matrix products: 68.2 us -> none  [the longest x1 9.35 us: attend_back(): jnp.dot(onehot.T, value_terms.reshape(-1, tile_width), precision=lax.Prec...]
    reshape x12 -> x0, local copies, waits for them, and re-layouts: 64.3 us -> none  [the longest x4 22.6 us: gather_blocks(): gathered = source.reshape(-1, block_len, head_count, head_dim)[listed]]
    reduce_scatter x1 -> x0, waiting for transfers between devices: 45.4 us -> none  [shards(): lax.psum_scatter(key_value_terms.astype(jnp.bfloat16), 'tm', scatter_dime...]
    psum x1 -> x0, waiting for transfers between devices: 42.8 us -> none  [shards(): lax.psum(output_part.astype(jnp.bfloat16), 'head').astype(jnp.float32)]
    another operation x34 -> x0, local copies, waits for them, and re-layouts: 33 us -> none  [the longest x33 24.5 us: conv_apply(): jnp.stack(taps_grad)]
  transfers between devices with their start and end apart: 7 -> 0, of which waited for: 6 -> 0; matrix products, arithmetic and copies ran while one was open for 14% -> 0% of each run, Pallas kernels for 0% -> 0%
where the time goes in v1:
time: 155 us; the launch traced here: 153 us
  Pallas kernels  140 us (90%)
  local copies, waits for them, and re-layouts  9.93 us (6%)
  other arithmetic  1.75 us (1%)
    pallas_call x1, Pallas kernels, finish(): pl.pallas_call(finish_kernel, out_shape=(jax.ShapeDtypeStruct((T, C), BF)...  66.9 us
    pallas_call x1, Pallas kernels, attention(): pl.pallas_call(attention_kernel, out_shape=(jax.ShapeDtypeStruct((4, HD,...  42.6 us
    pallas_call x1, Pallas kernels, project(): pl.pallas_call(project_kernel, out_shape=(jax.ShapeDtypeStruct((8, 2 * HD...  31 us
    unnamed x19, local copies, waits for them, and re-layouts  7.96 us

profile of v1, /device:TPU:1, one launch (start us, length us, event | category | flops | bytes accessed | tf_op | source)
XLA Modules:
  0.0 152.9 jit_solution(7961422890594754792)
XLA Ops:
  0.7 0.1 add_convert_fusion.qblock
  0.7 0.7 fusion.3
  1.4 0.1 slice_reduce_fusion
  1.5 0.1 broadcast_in_dim.33
  1.6 0.1 convert_element_type.30
  1.7 0.9 fusion
  2.6 0.1 broadcast_in_dim.35
  2.7 0.1 convert_element_type.33
  2.8 0.1 select_select_fusion.meta
  2.8 0.0 copy-start
  2.9 1.3 copy-done
  4.1 0.0 copy-start.6
  4.1 0.9 copy-done.6
  5.0 31.0 %project_exchange.1 = (bf16[8,192,384]{2,1,0:T(8,128)(2,1)S(1)}, bf16[4,208,384]{2,1,0:T(8,128)(2,1)S(1)}, bf16[1536,384]{1,0:T(8,128)(2,1)S(1)}, bf16[1536,384]{1,0:T(8,128)(2,1)S(1)}) custom-call(bf16[384,1536]{1,0:T(8,128)(2,1)S(1)} %bitcast.7, bf16[384,1536]{1,0:T(8,128)(2,1)} %bitcast.9, bf16[4,1536,384]{2,1,0:T(8,128)(2,1)} %w.1, ...), custom_call_target="tpu_custom_call" | custom-call | tf_op jit(solution)/shard_map/project_exchange/pallas_call | solution.py:132
  36.0 0.0 copy-start.3
  36.0 1.0 copy-done.3
  37.0 0.0 copy-start.4
  37.0 1.0 copy-done.4
  38.0 0.0 copy-start.7
  38.0 42.6 %attention_both.1 = (bf16[4,96,384]{2,1,0:T(8,128)(2,1)S(1)}, bf16[4,96,384]{2,1,0:T(8,128)(2,1)S(1)}, bf16[8,192,384]{2,1,0:T(8,128)(2,1)S(1)}) custom-call(bf16[8,192,384]{2,1,0:T(8,128)(2,1)S(1)} %get-tuple-element.15.kv, bf16[4,208,384]{2,1,0:T(8,128)(2,1)S(1)} %get-tuple-element.16.qd, f32[4,384]{1,0:T(4,128)S(1)} %add_convert_fusion.qblock), custom_call_target="tpu_custom_call" | custom-call | tf_op jit(solution)/shard_map/attention_both/pallas_call | solution.py:253
  80.6 0.0 copy-start.5
  80.6 1.0 copy-done.5
  81.6 0.0 copy-start.1
  81.6 0.0 copy-start.2
  81.6 1.5 %slice_bitcast_fusion.w3 = bf16[1536,384]{1,0:T(8,128)(2,1)S(1)} fusion(bf16[4,1536,384]{2,1,0:T(8,128)(2,1)} %w.1), kind=kLoop, calls=%fused_computation | loop fusion | bytes 2359296 | tf_op jit(solution)/shard_map/squeeze | solution.py:528
  83.2 0.0 copy-done.7
  83.2 0.1 copy-done.1
  83.3 0.4 copy-done.2
  83.6 66.9 %finish_exchange.1 = (bf16[384,1536]{1,0:T(8,128)(2,1)S(1)}, f32[4,48,384]{2,1,0:T(8,128)S(1)}, f32[1,1536]{1,0:T(1,128)S(1)}) custom-call(bf16[384,1536]{1,0:T(8,128)(2,1)S(1)} %bitcast.8, bf16[384,1536]{1,0:T(8,128)(2,1)S(1)} %bitcast.10, bf16[1536,384]{1,0:T(8,128)(2,1)S(1)} %slice_bitcast_fusion.w3, bf16[32,1536]{1,0:T(8,128)(2,1)S(1)} %copy-done.7, ...), custom_call_target="tpu_custom_call" | custom-call | tf_op jit(solution)/shard_map/finish_exchange/pallas_call | solution.py:476
  150.5 1.0 copy.16
  151.6 0.7 copy.17
  152.3 0.6 copy.18
  (4 shorter events, 0.0 us)
Async XLA Ops:
  2.8 1.3 copy-start
  4.1 0.9 copy-start.6
  36.0 1.0 copy-start.3
  37.0 1.0 copy-start.4
  38.0 45.2 %copy-start.7 = (bf16[32,1536]{1,0:T(8,128)(2,1)S(1)}, bf16[32,1536]{1,0:T(8,128)(2,1)}, u32[]{:S(2)}) copy-start(bf16[32,1536]{1,0:T(8,128)(2,1)} %taps.3) | copy-start | bytes 294916
  80.6 1.0 copy-start.5
  81.6 1.6 %copy-start.1 = (bf16[1,384,1536]{2,1,0:T(8,128)(2,1)S(1)}, bf16[1,384,1536]{2,1,0:T(8,128)(2,1)}, u32[]{:S(2)}) copy-start(bf16[1,384,1536]{2,1,0:T(8,128)(2,1)} %param.5) | copy-start | bytes 3538948
  81.6 2.0 %copy-start.2 = (bf16[1,384,1536]{2,1,0:T(8,128)(2,1)S(1)}, bf16[1,384,1536]{2,1,0:T(8,128)(2,1)}, u32[]{:S(2)}) copy-start(bf16[1,384,1536]{2,1,0:T(8,128)(2,1)} %param.9) | copy-start | bytes 3538948

commit v2 on v1

--- a/solution.py
+++ b/solution.py
@@ -13,7 +13,7 @@
 C = 1536
 F = 384
 NKB = 48
-QC = 256
+QC = 768
 MESH = pl.DeviceIdType.MESH
 BF = jnp.bfloat16
 F32 = jnp.float32
@@ -197,7 +197,7 @@
             st[rows, :] = jnp.concatenate(parts, axis=0)
             return top
 
-        top = lax.fori_loop(0, 8, scores, jnp.full((8, QC), -jnp.inf, F32))
+        top = lax.fori_loop(0, 8, scores, jnp.full((8, QC), -jnp.inf, F32), unroll=8)
         top = jnp.max(top, axis=0, keepdims=True) * c2
 
         def weigh(t, carry):
@@ -211,7 +211,7 @@
             return total, o
 
         total, o = lax.fori_loop(
-            0, 8, weigh, (jnp.zeros((8, QC), F32), jnp.zeros((HD, QC), F32))
+            0, 8, weigh, (jnp.zeros((8, QC), F32), jnp.zeros((HD, QC), F32)), unroll=8
         )
         inverse = 1.0 / jnp.sum(total, axis=0, keepdims=True)
         o = (o * inverse).astype(BF)
@@ -233,7 +233,7 @@
                 kt[:, pl.ds(pl.multiple_of(t * T, T), T)], ds, preferred_element_type=F32
             )
 
-        dq = lax.fori_loop(0, 8, back, jnp.zeros((HD, QC), F32))
+        dq = lax.fori_loop(0, 8, back, jnp.zeros((HD, QC), F32), unroll=8)
         dqn[:, lanes] = (dq * scale).astype(BF)
         return carry
 

time: 155 us -> 131 us (0.85)
  Pallas kernels: 140 us -> 116 us
    pallas_call x1, Pallas kernels: 42.6 us -> 18 us  [attention(): pl.pallas_call(attention_kernel, out_shape=(jax.ShapeDtypeStruct((4, HD,...]
where the time goes in v2:
time: 131 us; the launch traced here: 128 us
  Pallas kernels  116 us (89%)
  local copies, waits for them, and re-layouts  9.93 us (8%)
  other arithmetic  1.75 us (1%)
    pallas_call x1, Pallas kernels, finish(): pl.pallas_call(finish_kernel, out_shape=(jax.ShapeDtypeStruct((T, C), BF)...  66.9 us
    pallas_call x1, Pallas kernels, project(): pl.pallas_call(project_kernel, out_shape=(jax.ShapeDtypeStruct((8, 2 * HD...  31 us
    pallas_call x1, Pallas kernels, attention(): pl.pallas_call(attention_kernel, out_shape=(jax.ShapeDtypeStruct((4, HD,...  18 us
    unnamed x19, local copies, waits for them, and re-layouts  7.96 us

profile of v2, /device:TPU:1, one launch (start us, length us, event | category | flops | bytes accessed | tf_op | source)
XLA Modules:
  0.0 128.3 jit_solution(5234550414676991585)
XLA Ops:
  0.7 0.1 add_convert_fusion.qblock
  0.7 0.7 fusion.3
  1.4 0.1 slice_reduce_fusion
  1.5 0.1 broadcast_in_dim.33
  1.6 0.1 convert_element_type.30
  1.7 0.9 fusion
  2.6 0.1 broadcast_in_dim.35
  2.7 0.1 convert_element_type.33
  2.8 0.1 select_select_fusion.meta
  2.8 0.0 copy-start
  2.9 1.3 copy-done
  4.1 0.0 copy-start.6
  4.1 0.9 copy-done.6
  5.0 31.0 %project_exchange.1 = (bf16[8,192,384]{2,1,0:T(8,128)(2,1)S(1)}, bf16[4,208,384]{2,1,0:T(8,128)(2,1)S(1)}, bf16[1536,384]{1,0:T(8,128)(2,1)S(1)}, bf16[1536,384]{1,0:T(8,128)(2,1)S(1)}) custom-call(bf16[384,1536]{1,0:T(8,128)(2,1)S(1)} %bitcast.7, bf16[384,1536]{1,0:T(8,128)(2,1)} %bitcast.9, bf16[4,1536,384]{2,1,0:T(8,128)(2,1)} %w.1, ...), custom_call_target="tpu_custom_call" | custom-call | tf_op jit(solution)/shard_map/project_exchange/pallas_call | solution.py:132
  36.0 0.0 copy-start.3
  36.0 1.0 copy-done.3
  37.0 0.0 copy-start.4
  37.0 1.0 copy-done.4
  38.0 0.0 copy-start.7
  38.0 18.0 %attention_both.1 = (bf16[4,96,384]{2,1,0:T(8,128)(2,1)S(1)}, bf16[4,96,384]{2,1,0:T(8,128)(2,1)S(1)}, bf16[8,192,384]{2,1,0:T(8,128)(2,1)S(1)}) custom-call(bf16[8,192,384]{2,1,0:T(8,128)(2,1)S(1)} %get-tuple-element.15.kv, bf16[4,208,384]{2,1,0:T(8,128)(2,1)S(1)} %get-tuple-element.16.qd, f32[4,384]{1,0:T(4,128)S(1)} %add_convert_fusion.qblock), custom_call_target="tpu_custom_call" | custom-call | tf_op jit(solution)/shard_map/attention_both/pallas_call | solution.py:253
  56.1 0.0 copy-start.5
  56.1 1.0 copy-done.5
  57.1 0.0 copy-start.1
  57.1 0.0 copy-start.2
  57.1 1.5 %slice_bitcast_fusion.w3 = bf16[1536,384]{1,0:T(8,128)(2,1)S(1)} fusion(bf16[4,1536,384]{2,1,0:T(8,128)(2,1)} %w.1), kind=kLoop, calls=%fused_computation | loop fusion | bytes 2359296 | tf_op jit(solution)/shard_map/squeeze | solution.py:528
  58.6 0.0 copy-done.7
  58.6 0.1 copy-done.1
  58.7 0.4 copy-done.2
  59.1 66.9 %finish_exchange.1 = (bf16[384,1536]{1,0:T(8,128)(2,1)S(1)}, f32[4,48,384]{2,1,0:T(8,128)S(1)}, f32[1,1536]{1,0:T(1,128)S(1)}) custom-call(bf16[384,1536]{1,0:T(8,128)(2,1)S(1)} %bitcast.8, bf16[384,1536]{1,0:T(8,128)(2,1)S(1)} %bitcast.10, bf16[1536,384]{1,0:T(8,128)(2,1)S(1)} %slice_bitcast_fusion.w3, bf16[32,1536]{1,0:T(8,128)(2,1)S(1)} %copy-done.7, ...), custom_call_target="tpu_custom_call" | custom-call | tf_op jit(solution)/shard_map/finish_exchange/pallas_call | solution.py:476
  126.0 1.0 copy.16
  127.0 0.7 copy.17
  127.7 0.6 copy.18
  (4 shorter events, 0.0 us)
Async XLA Ops:
  2.8 1.3 copy-start
  4.1 0.9 copy-start.6
  36.0 1.0 copy-start.3
  37.0 1.0 copy-start.4
  38.0 20.6 %copy-start.7 = (bf16[32,1536]{1,0:T(8,128)(2,1)S(1)}, bf16[32,1536]{1,0:T(8,128)(2,1)}, u32[]{:S(2)}) copy-start(bf16[32,1536]{1,0:T(8,128)(2,1)} %taps.3) | copy-start | bytes 294916
  56.1 1.0 copy-start.5
  57.1 1.6 %copy-start.1 = (bf16[1,384,1536]{2,1,0:T(8,128)(2,1)S(1)}, bf16[1,384,1536]{2,1,0:T(8,128)(2,1)}, u32[]{:S(2)}) copy-start(bf16[1,384,1536]{2,1,0:T(8,128)(2,1)} %param.5) | copy-start | bytes 3538948
  57.1 2.0 %copy-start.2 = (bf16[1,384,1536]{2,1,0:T(8,128)(2,1)S(1)}, bf16[1,384,1536]{2,1,0:T(8,128)(2,1)}, u32[]{:S(2)}) copy-start(bf16[1,384,1536]{2,1,0:T(8,128)(2,1)} %param.9) | copy-start | bytes 3538948

commit v3 on v0

v3 whole, which is shorter than its diff:
```python
import types

import jax
import jax.numpy as jnp
from jax import lax
from jax.experimental import pallas as pl
from jax.experimental.pallas import tpu as pltpu
from jax.sharding import PartitionSpec as P

HD = 96
BLK = 64
KW = 32
HALF = KW // 2
T = 384
C = 1536
F = 384
Q = 4 * T
QC = 768
MESH = pl.DeviceIdType.MESH
BF = jnp.bfloat16
F32 = jnp.float32
SCALE = HD**-0.5
NT = (((1,), (1,)), ((), ()))


def dma(*shape):
    return pltpu.SemaphoreType.DMA(shape)


def vm(dtype, *shape):
    return pltpu.VMEM(shape, dtype)


SCRATCH = dict(
    frames=vm(BF, T, C), cot=vm(BF, T, C), w=vm(BF, 4, C, F), taps=vm(BF, KW, C), pattern=vm(jnp.int32, 1, 6, 12),
    in_sem=dma(9),
    upad=vm(F32, T + 2 * HALF, C), uhalo=vm(BF, 2, HALF, C), tapsf=vm(F32, KW, C),
    bg=vm(BF, T, C), bg_t=vm(BF, C, T), frames_t=vm(BF, C, T), uh_s=dma(2), uh_r=dma(2),
    q_s=vm(BF, 4, HD + 16, T), k_s=vm(BF, 4, HD, T), v_s=vm(BF, 4, HD, T), d_s=vm(BF, 4, HD, T),
    q_r=vm(BF, 4, HD + 16, T), d_r=vm(BF, 4, HD, T), k_r=vm(BF, 8, HD, T), v_r=vm(BF, 8, HD, T),
    qs=dma(4), qr=dma(4), ks=dma(4), kr=dma(4), vs=dma(4), vr=dma(4), ds=dma(4), dr=dma(4),
    fks=dma(4), fkr=dma(4), fvs=dma(4), fvr=dma(4),
    kn=vm(BF, 8, T, HD), vn=vm(BF, 8, T, HD), qt=vm(BF, HD, Q), qn=vm(BF, Q, HD), dt=vm(BF, HD, Q), dn=vm(BF, Q, HD),
    live=vm(F32, 64, Q), st=vm(F32, 8, T, QC), et=vm(BF, 8, T, Q), dsb=vm(BF, 2, T, Q), dq=vm(F32, HD, Q),
    inverse=vm(F32, 1, Q), delta=vm(F32, 1, Q),
    o_s=vm(BF, 4, HD, T), dq_s=vm(BF, 4, HD, T), part_s=vm(BF, 4, 2 * HD, T), part_r=vm(BF, 4, 2 * HD, T),
    dkv_s=vm(BF, 4, 2 * HD, T), mix_r=vm(BF, 4, HD, T), dq_r=vm(BF, 4, HD, T), dkv_r=vm(BF, 4, 2 * HD, T),
    os=dma(4), orr=dma(4), dqs=dma(4), dqr=dma(4), ps=dma(4), pr=dma(4), dkvs=dma(4), dkvr=dma(4),
    op_s=vm(BF, 3, T, F), op_r=vm(BF, 3, T, F), ops=dma(3), opr=dma(3),
    rpad=vm(F32, T + 2 * HALF, F), res=vm(BF, T, F), rhalo=vm(BF, 2, HALF, F), enc=vm(BF, T, F),
    rh_s=dma(2), rh_r=dma(2), es=dma(4), er=dma(4),
    kacc=vm(F32, KW, 8, F), kg=vm(F32, KW, 1, F), kgr=vm(F32, KW, 1, F), kgy=vm(F32, 4, 1, F),
    kgs=dma(32), kgrs=dma(32), kys=dma(4), kyr=dma(4),
    g_s=vm(BF, 4, 2, F, F), g_r=vm(BF, 4, 2, F, F), gs=dma(4), gr=dma(4),
    h1=vm(BF, 4, 16, 48, F), s1=vm(BF, 4, 3, 4, 48, F), h2=vm(BF, 4, 4, 48, F), s2=vm(BF, 4, 3, 48, F),
    s1s=dma(4, 4), s1r=dma(4, 4), s2s=dma(4, 4), s2r=dma(4, 4),
)


def remote(src, dst, ssem, rsem, device):
    return pltpu.make_async_remote_copy(
        src_ref=src, dst_ref=dst, send_sem=ssem, recv_sem=rsem, device_id=device, device_id_type=MESH
    )


class Either:
    def __init__(self, here, src, dst, ssem, rsem, device):
        self.here = here
        self.local = pltpu.make_async_copy(src, dst, rsem)
        self.far = remote(src, dst, ssem, rsem, device)

    def start(self):
        pl.when(self.here)(lambda: self.local.start())
        pl.when(jnp.logical_not(self.here))(lambda: self.far.start())

    def wait(self):
        pl.when(self.here)(lambda: self.local.wait())
        pl.when(jnp.logical_not(self.here))(lambda: self.far.wait())


def go(copy):
    copy.start()
    return copy


def wait_all(copies):
    for c in copies:
        c.wait()


def tap_terms(window, offsets):
    for r in range(8):
        shifted = window[r : r + 88] if r else window
        for a in range(5):
            o = 8 * a + r
            if o in offsets:
                yield offsets[o], shifted[8 * a : 8 * a + 64]


def aligned(start, size, by):
    return pl.ds(pl.multiple_of(start, by), size)


def layer_kernel(frames_h, w_h, taps_h, pattern_h, cot_h, enc_out, pg_out, kg_out, *scratch):
    s = types.SimpleNamespace(**dict(zip(SCRATCH, scratch)))
    dp, tm, hd = lax.axis_index("dp"), lax.axis_index("tm"), lax.axis_index("head")
    zl, core = dp // 2, lax.rem(dp, 2)
    x, zh = tm // 2, lax.rem(tm, 2)
    z = zh * 2 + zl
    me = dp * 8 + tm
    around = lambda k: lax.rem(x + k, 4)
    at_tm = lambda k: (dp, lax.rem(tm + k, 8), hd)
    at_x = lambda k: (dp, around(k) * 2 + zh, hd)
    at_y = lambda k: (dp, tm, lax.rem(hd + k, 4))
    sibling = (zl * 2 + 1 - core, tm, hd)

    def at_z(k):
        to = lax.rem(z + k, 4)
        return (lax.rem(to, 2) * 2 + core, x * 2 + to // 2, hd)

    def at_plane(k):
        to = lax.rem(me + k, 32)
        return (to // 8, lax.rem(to, 8), hd)

    def swapped(k, src, dst, ssem, rsem):
        device = (zl * 2 + zh, around(k) * 2 + core, hd)
        if k:
            return go(remote(src, dst, ssem.at[k], rsem.at[k], device))
        return go(Either(zh == core, src, dst, ssem.at[0], rsem.at[0], device))

    load = [
        go(pltpu.make_async_copy(a, b, s.in_sem.at[i]))
        for i, (a, b) in enumerate(
            [
                (frames_h.at[0], s.frames),
                (w_h.at[1], s.w.at[1]),
                (w_h.at[0], s.w.at[0]),
                (w_h.at[2], s.w.at[2]),
                (cot_h.at[0], s.cot),
                (taps_h, s.taps),
                (pattern_h, s.pattern),
                (w_h.at[3], s.w.at[3]),
            ]
        )
    ]
    barrier = pltpu.get_barrier_semaphore()
    others = [at_plane(k) for k in range(1, 32)] + [at_y(k) for k in range(1, 4)]
    for device in others:
        pl.semaphore_signal(barrier, inc=1, device_id=device, device_id_type=MESH)

    def projected(rows, p):
        return jnp.dot(rows, s.w[p], preferred_element_type=F32).astype(BF).T

    load[0].wait()
    load[1].wait()
    y = projected(s.frames[...], 1)
    for h in range(4):
        s.k_s[h] = y[h * HD : (h + 1) * HD]
    pl.semaphore_wait(barrier, len(others))
    k_c = [swapped(k, s.k_s.at[around(k)], s.k_r.at[x], s.ks, s.kr) for k in (1, 2, 3, 0)]
    load[4].wait()
    halos = [
        go(remote(s.cot.at[T - HALF : T], s.uhalo.at[0], s.uh_s.at[0], s.uh_r.at[0], at_tm(1))),
        go(remote(s.cot.at[0:HALF], s.uhalo.at[1], s.uh_s.at[1], s.uh_r.at[1], at_tm(7))),
    ]
    load[2].wait()
    load[6].wait()
    y = projected(s.frames[...], 0)
    blocks = s.pattern[0]
    block_of = lax.broadcasted_iota(jnp.int32, (6, T), 1) // BLK == lax.broadcasted_iota(jnp.int32, (6, T), 0)
    spread = lambda column: jnp.sum(jnp.where(block_of, column.astype(F32), 0.0), axis=0, keepdims=True)
    phase = spread(blocks[:, 0:1])
    count = spread(jnp.sum((blocks >= 0).astype(F32), axis=1, keepdims=True))
    row = lax.broadcasted_iota(jnp.int32, (16, T), 0)
    meta = jnp.where(row == 0, phase, jnp.where(row == 1, count, 0.0)).astype(BF)
    for h in range(4):
        s.q_s[h, 0:HD] = y[h * HD : (h + 1) * HD]
        s.q_s[h, HD:] = meta
    q_c = [swapped(k, s.q_s.at[around(k)], s.q_r.at[x], s.qs, s.qr) for k in (1, 2, 3, 0)]
    load[3].wait()
    y = projected(s.frames[...], 2)
    for h in range(4):
        s.v_s[h] = y[h * HD : (h + 1) * HD]
    v_c = [swapped(k, s.v_s.at[around(k)], s.v_r.at[x], s.vs, s.vr) for k in (1, 2, 3, 0)]

    load[5].wait()
    s.tapsf[...] = s.taps[...].astype(F32)
    s.upad[HALF : HALF + T] = s.cot[...].astype(F32)
    wait_all(halos)
    s.upad[0:HALF] = jnp.where(tm > 0, s.uhalo[0].astype(F32), 0.0)
    s.upad[HALF + T :] = jnp.where(tm < 7, s.uhalo[1].astype(F32), 0.0)

    def conv_back(it, carry):
        i, l = it // 12, lax.rem(it, 12)
        lanes = aligned(l * 128, 128, 128)
        window = s.upad[aligned(i * 64, 96, 64), lanes]
        acc = window[HALF : HALF + 64]
        for j, rows in tap_terms(window, {2 * HALF - j: j for j in range(KW)}):
            acc = acc + s.tapsf[j : j + 1, lanes] * rows
        s.bg[aligned(i * 64, 64, 64), lanes] = acc.astype(BF)
        return carry

    lax.fori_loop(0, 72, conv_back, 0)
    load[7].wait()
    y = projected(s.bg[...], 3)
    for h in range(4):
        s.d_s[h] = y[h * HD : (h + 1) * HD]
    d_c = [swapped(k, s.d_s.at[around(k)], s.d_r.at[x], s.ds, s.dr) for k in (1, 2, 3, 0)]

    def forward(k, copy, buf, ssem, rsem):
        copy.wait()
        src = lax.rem(x + 4 - k, 4)
        return go(remote(buf.at[src], buf.at[4 + src], ssem.at[k], rsem.at[k], sibling))

    fk_c = [forward(k, c, s.k_r, s.fks, s.fkr) for k, c in zip((1, 2, 3, 0), k_c)]
    wait_all(q_c)
    for a in range(4):
        lanes = slice(a * T, (a + 1) * T)
        s.qt[:, lanes] = s.q_r[a, 0:HD]
        s.qn[lanes, :] = s.q_r[a, 0:HD].T
        got = s.q_r[a, HD:].astype(F32)
        row = lax.broadcasted_iota(jnp.int32, (64, T), 0)
        tile = row // 8
        owner = lax.rem(tile, 4) * 2 + jnp.where(tile < 4, core, 1 - core)
        key_block = owner * 6 + lax.rem(row, 8)
        query_block = (a * 2 + core) * 6 + lax.broadcasted_iota(jnp.int32, (64, T), 1) // BLK
        far = (lax.rem(key_block, 4).astype(F32) == got[0:1]) & ((key_block // 4).astype(F32) < got[1:2])
        near = jnp.abs(key_block - query_block) < 2
        s.live[:, lanes] = jnp.where(far | near, 1.0, 0.0)
    for t in range(4):
        s.kn[t] = s.k_r[t].T
    fv_c = [forward(k, c, s.v_r, s.fvs, s.fvr) for k, c in zip((1, 2, 3, 0), v_c)]
    wait_all(fk_c)
    for t in range(4, 8):
        s.kn[t] = s.k_r[t].T

    for c in range(Q // QC):
        lanes = slice(c * QC, (c + 1) * QC)
        q_t = s.qt[:, lanes]

        def scores(t, top):
            sc = jnp.dot(s.kn[t], q_t, preferred_element_type=F32)
            mask = s.live[aligned(t * 8, 8, 8), lanes]
            for b in range(6):
                part = jnp.where(mask[b : b + 1] > 0.5, sc[b * BLK : (b + 1) * BLK], -1e30)
                top = jnp.maximum(top, jnp.max(part.reshape(8, 8, QC), axis=0))
                s.st[t, b * BLK : (b + 1) * BLK] = part
            return top

        top = lax.fori_loop(0, 8, scores, jnp.full((8, QC), -jnp.inf, F32), unroll=8)
        c2 = SCALE * 1.4426950408889634
        top = jnp.max(top, axis=0, keepdims=True) * c2
        if c == 0:
            wait_all(fv_c)

        def weigh(t, carry):
            total, o = carry
            e = jnp.exp2(s.st[t] * c2 - top)
            total = total + jnp.sum(e.reshape(T // 8, 8, QC), axis=0)
            eb = e.astype(BF)
            s.et[t, :, lanes] = eb
            return total, o + jnp.dot(s.v_r[t], eb, preferred_element_type=F32)

        total, o = lax.fori_loop(
            0, 8, weigh, (jnp.zeros((8, QC), F32), jnp.zeros((HD, QC), F32)), unroll=8
        )
        inverse = 1.0 / jnp.sum(total, axis=0, keepdims=True)
        s.inverse[:, lanes] = inverse
        o = (o * inverse).astype(BF)
        for a in range(2):
            s.o_s[c * 2 + a] = o[:, a * T : (a + 1) * T]
    o_c = [swapped(k, s.o_s.at[around(k)], s.mix_r.at[x], s.os, s.orr) for k in (1, 2, 3, 0)]

    wait_all(d_c)
    for a in range(4):
        lanes = slice(a * T, (a + 1) * T)
        d = s.d_r[a].astype(F32)
        inverse = s.inverse[:, lanes]
        s.delta[:, lanes] = jnp.sum(d * s.o_s[a].astype(F32), axis=0, keepdims=True) * inverse
        d = (d * inverse).astype(BF)
        s.dt[:, lanes] = d
        s.dn[lanes, :] = d.T
    for t in range(8):
        s.vn[t] = s.v_r[t].T
    s.dq[...] = jnp.zeros_like(s.dq)

    def back(first, k, slot):
        t = first + around(k)
        for c in range(Q // QC):
            lanes = slice(c * QC, (c + 1) * QC)
            dp_ = jnp.dot(s.vn[t], s.dt[:, lanes], preferred_element_type=F32)
            s.dsb[slot, :, lanes] = (s.et[t, :, lanes].astype(F32) * (dp_ - s.delta[:, lanes])).astype(BF)
        dk = jnp.dot(s.dsb[slot], s.qn[...], preferred_element_type=F32) * SCALE
        dv = jnp.dot(s.et[t], s.dn[...], preferred_element_type=F32)
        s.dq[...] += jnp.dot(s.k_r[t], s.dsb[slot], preferred_element_type=F32)
        return dk, dv

    def back_pair(first, ks, out):
        for slot, k in enumerate(ks):
            dk, dv = back(first, k, slot)
            out[around(k), 0:HD] = dk.astype(BF).T
            out[around(k), HD:] = dv.astype(BF).T

    p_c = {}
    for ks in ((1, 2), (3, 0)):
        back_pair(4, ks, s.part_s)
        for k in ks:
            i = around(k)
            p_c[k] = go(remote(s.part_s.at[i], s.part_r.at[i], s.ps.at[k], s.pr.at[k], sibling))

    wait_all(o_c)
    mixed = s.mix_r[...].reshape(F, T).T
    op_c = []
    for k in range(1, 4):
        rows = aligned(lax.rem(hd + k, 4) * F, F, F)
        s.op_s[k - 1] = lax.dot_general(mixed, s.w[3, rows, :], NT, preferred_element_type=F32).astype(BF)
        op_c.append(go(remote(s.op_s.at[k - 1], s.op_r.at[k - 1], s.ops.at[k - 1], s.opr.at[k - 1], at_y(k))))
    s.frames_t[...] = s.frames[...].T
    s.bg_t[...] = s.bg[...].T

    def away(p, left, right):
        for l in range(2):
            rows = aligned((l * 2 + 1 - core) * F, F, F)
            s.g_s[p, l] = jnp.dot(left[rows, :], right, preferred_element_type=F32).astype(BF)
        return go(remote(s.g_s.at[p], s.g_r.at[p], s.gs.at[p], s.gr.at[p], sibling))

    def keep(p, left, right, copy, by_x):
        copy.wait()
        for l in range(2):
            rows = aligned((l * 2 + core) * F, F, F)
            g = jnp.dot(left[rows, :], right, preferred_element_type=F32) + s.g_r[p, l].astype(F32)
            g = g.astype(BF)
            for xo in range(4):
                for h in range(2):
                    piece = g[xo * 96 + h * 48 : xo * 96 + h * 48 + 48]
                    s.h1[p, xo * 4 + h * 2 + l if by_x else (h * 2 + l) * 4 + xo] = piece
        out = []
        for k in range(1, 4):
            to = lax.rem((x if by_x else z) + k, 4)
            device = at_x(k) if by_x else at_z(k)
            out.append(
                go(remote(s.h1.at[p, pl.ds(to * 4, 4)], s.s1.at[p, k - 1], s.s1s.at[p, k], s.s1r.at[p, k], device))
            )
        return out

    def second(p, copies, by_x):
        wait_all(copies)
        own = s.h1[p, pl.ds((x if by_x else z) * 4, 4)].astype(F32)
        for k in range(3):
            own = own + s.s1[p, k].astype(F32)
        s.h2[p] = own.astype(BF)
        out = []
        for k in range(1, 4):
            to = lax.rem((z if by_x else x) + k, 4)
            device = at_z(k) if by_x else at_x(k)
            out.append(go(remote(s.h2.at[p, to], s.s2.at[p, k - 1], s.s2s.at[p, k], s.s2r.at[p, k], device)))
        return out

    def last(p, copies, by_x):
        wait_all(copies)
        own = s.h2[p, z if by_x else x].astype(F32)
        for k in range(3):
            own = own + s.s2[p, k].astype(F32)
        pg_out[p] = own

    by_x = (False, False, True, True)
    g3 = away(3, s.bg_t, mixed)

    dkv_c = []
    for n, ks in enumerate(((1, 2), (3, 0))):
        for slot, k in enumerate(ks):
            dk, dv = back(0, k, slot)
            p_c[k].wait()
            i = around(k)
            s.dkv_s[i, 0:HD] = (dk.T + s.part_r[i, 0:HD].astype(F32)).astype(BF)
            s.dkv_s[i, HD:] = (dv.T + s.part_r[i, HD:].astype(F32)).astype(BF)
        for k in ks:
            dkv_c.append(swapped(k, s.dkv_s.at[around(k)], s.dkv_r.at[x], s.dkvs, s.dkvr))
        if n == 0:
            r3 = keep(3, s.bg_t, mixed, g3, by_x[3])
    for a in range(4):
        s.dq_s[a] = (s.dq[:, a * T : (a + 1) * T] * SCALE).astype(BF)
    dq_c = [swapped(k, s.dq_s.at[around(k)], s.dq_r.at[x], s.dqs, s.dqr) for k in (1, 2, 3, 0)]

    summed = lax.dot_general(mixed, s.w[3, aligned(hd * F, F, F), :], NT, preferred_element_type=F32)
    wait_all(op_c)
    for k in range(3):
        summed = summed + s.op_r[k].astype(F32)
    mine = aligned(hd * F, F, 128)
    s.res[...] = (s.frames[:, mine].astype(F32) + summed).astype(BF)
    halos = [
        go(remote(s.res.at[T - HALF : T], s.rhalo.at[0], s.rh_s.at[0], s.rh_r.at[0], at_tm(1))),
        go(remote(s.res.at[0:HALF], s.rhalo.at[1], s.rh_s.at[1], s.rh_r.at[1], at_tm(7))),
    ]

    wait_all(dkv_c)
    dk = s.dkv_r[:, 0:HD].reshape(F, T).T
    g1 = away(1, s.frames_t, dk)
    dv = s.dkv_r[:, HD:].reshape(F, T).T
    g2 = away(2, s.frames_t, dv)
    wait_all(dq_c)
    dq = s.dq_r[...].reshape(F, T).T
    g0 = away(0, s.frames_t, dq)
    r1 = keep(1, s.frames_t, dk, g1, by_x[1])
    r2 = keep(2, s.frames_t, dv, g2, by_x[2])
    r0 = keep(0, s.frames_t, dq, g0, by_x[0])
    t3 = second(3, r3, by_x[3])

    s.kacc[...] = jnp.zeros_like(s.kacc)
    s.rpad[HALF : HALF + T] = s.res[...].astype(F32)
    wait_all(halos)
    s.rpad[0:HALF] = jnp.where(tm > 0, s.rhalo[0].astype(F32), 0.0)
    s.rpad[HALF + T :] = jnp.where(tm < 7, s.rhalo[1].astype(F32), 0.0)

    def conv(it, carry):
        i, l = it // 3, lax.rem(it, 3)
        lanes = aligned(l * 128, 128, 128)
        whole = aligned(hd * F + l * 128, 128, 128)
        window = s.rpad[aligned(i * 64, 96, 64), lanes]
        up = s.cot[aligned(i * 64, 64, 64), whole].astype(F32)
        acc = window[HALF : HALF + 64]
        for j, rows in tap_terms(window, {j: j for j in range(KW)}):
            acc = acc + s.tapsf[j : j + 1, whole] * rows
            s.kacc[j, :, lanes] += jnp.sum((up * rows).reshape(8, 8, 128), axis=0)
        s.enc[aligned(i * 64, 64, 64), lanes] = acc.astype(BF)
        return carry

    lax.fori_loop(0, 18, conv, 0)
    e_c = [go(remote(s.enc, enc_out.at[0, :, mine], s.es.at[k], s.er.at[k], at_y(k))) for k in range(1, 4)]
    e_c.append(go(pltpu.make_async_copy(s.enc, enc_out.at[0, :, mine], s.in_sem.at[8])))
    for j in range(KW):
        s.kg[j] = jnp.sum(s.kacc[j], axis=0, keepdims=True)
    kg_c = []
    for k in range(1, 32):
        to = lax.rem(me + k, 32)
        kg_c.append(go(remote(s.kg.at[to], s.kgr.at[k], s.kgs.at[k], s.kgrs.at[k], at_plane(k))))

    t1 = second(1, r1, by_x[1])
    t2 = second(2, r2, by_x[2])
    t0 = second(0, r0, by_x[0])
    wait_all(kg_c)
    total = s.kg[me]
    for k in range(1, 32):
        total = total + s.kgr[k]
    s.kgy[hd] = total
    ky_c = [go(remote(s.kgy.at[hd], s.kgy.at[hd], s.kys.at[k], s.kyr.at[k], at_y(k))) for k in range(1, 4)]
    for p, t in ((3, t3), (1, t1), (2, t2), (0, t0)):
        last(p, t, by_x[p])
    wait_all(ky_c)
    for y in range(4):
        kg_out[:, y * F : (y + 1) * F] = s.kgy[y]
    wait_all(e_c)


def shards(frames, projections, kernel, pattern, cotangent):
    vmem = pl.BlockSpec(memory_space=pltpu.VMEM)
    anym = pl.BlockSpec(memory_space=pl.ANY)
    return pl.pallas_call(
        layer_kernel,
        out_shape=(
            jax.ShapeDtypeStruct((1, T, C), BF),
            jax.ShapeDtypeStruct((4, 48, F), F32),
            jax.ShapeDtypeStruct((1, C), F32),
        ),
        in_specs=[anym] * 5,
        out_specs=(anym, vmem, vmem),
        scratch_shapes=list(SCRATCH.values()),
        compiler_params=pltpu.CompilerParams(
            collective_id=0, has_side_effects=True, vmem_limit_bytes=60 << 20
        ),
        name="conformer_layer",
    )(frames, projections, kernel, pattern, cotangent)


def solution(mesh):
    placed = (
        P("dp", "tm", None),
        P(None, None, "head"),
        P(),
        P("dp", "tm", None),
        P("dp", "tm", None),
    )
    return jax.shard_map(
        shards,
        mesh=mesh,
        in_specs=placed,
        out_specs=(P("dp", "tm", None), P(None, ("dp", "tm"), "head"), P(("dp", "tm"), None)),
        check_vma=False,
    )
```

time: 605 us -> 106 us (0.18); the launches traced: 593 us -> 106 us
  waiting for transfers between devices: 286 us -> 0 us
  local copies, waits for them, and re-layouts: 158 us -> 4.99 us
  Pallas kernels: 0 us -> 101 us
  matrix products: 68.2 us -> 0 us
  other arithmetic: 58.4 us -> 0 us
  between operations: 16.1 us -> 0.66 us
  starting transfers between devices: 6.28 us -> 0 us
    all_gather x2 -> x0, waiting for transfers between devices: 101 us -> none  [the longest x1 53.7 us: shards(): lax.all_gather(key_rows, 'tm', axis=0, tiled=True)]
    pallas_call x0 -> x1, Pallas kernels: none -> 101 us  [shards(): pl.pallas_call(layer_kernel, out_shape=(jax.ShapeDtypeStruct((1, T, C), B...]
    unnamed x6 -> x0, waiting for transfers between devices: 92.3 us -> none
    dot_general x17 -> x0, matrix products: 68.2 us -> none  [the longest x1 9.35 us: attend_back(): jnp.dot(onehot.T, value_terms.reshape(-1, tile_width), precision=lax.Prec...]
    reshape x12 -> x0, local copies, waits for them, and re-layouts: 64.3 us -> none  [the longest x4 22.6 us: gather_blocks(): gathered = source.reshape(-1, block_len, head_count, head_dim)[listed]]
    reduce_scatter x1 -> x0, waiting for transfers between devices: 45.4 us -> none  [shards(): lax.psum_scatter(key_value_terms.astype(jnp.bfloat16), 'tm', scatter_dime...]
    psum x1 -> x0, waiting for transfers between devices: 42.8 us -> none  [shards(): lax.psum(output_part.astype(jnp.bfloat16), 'head').astype(jnp.float32)]
    another operation x34 -> x0, local copies, waits for them, and re-layouts: 33 us -> none  [the longest x33 24.5 us: conv_apply(): jnp.stack(taps_grad)]
  transfers between devices with their start and end apart: 7 -> 0, of which waited for: 6 -> 0; matrix products, arithmetic and copies ran while one was open for 14% -> 0% of each run, Pallas kernels for 0% -> 0%
where the time goes in v3:
time: 106 us
  Pallas kernels  101 us (95%)
  local copies, waits for them, and re-layouts  4.99 us (5%)
    pallas_call x1, Pallas kernels, shards(): pl.pallas_call(layer_kernel, out_shape=(jax.ShapeDtypeStruct((1, T, C), B...  101 us
    unnamed x8, local copies, waits for them, and re-layouts  4.99 us

profile of v3, /device:TPU:1, one launch (start us, length us, event | category | flops | bytes accessed | tf_op | source)
XLA Modules:
  0.0 106.2 jit_solution(8580709619783436963)
XLA Ops:
  0.6 1.3 %copy.8.pattern_h = s32[1,6,12]{2,1,0:T(8,128)} copy(s32[1,6,12]{2,0,1:T(1,128)} %param.8) | data formatting | bytes 576 | tf_op args[3]
  1.9 100.6 %conformer_layer.1 = (bf16[1,384,1536]{2,1,0:T(8,128)(2,1)}, f32[4,48,384]{2,1,0:T(8,128)}, f32[1,1536]{1,0:T(1,128)}) custom-call(bf16[1,384,1536]{2,1,0:T(8,128)(2,1)} %frames_h.1, bf16[4,1536,384]{2,1,0:T(8,128)(2,1)} %w_h.1, bf16[32,1536]{1,0:T(8,128)(2,1)} %taps_h.1, s32[1,6,12]{2,1,0:T(8,128)} %copy.8.pattern_h, bf16[1,384,1536]{2,1,0:T(8,128)(2,1)} %cot_h.1), custom_call_target="tpu_custom_call" | custom-call | tf_op jit(solution)/shard_map/conformer_layer/pallas_call | solution.py:458
  102.5 0.0 copy-start
  102.5 0.0 copy-start.1
  102.5 2.4 %copy.12 = bf16[1,384,1536]{2,1,0:T(8,128)(2,1)} copy(bf16[1,384,1536]{2,1,0:T(8,128)(2,1)} %get-tuple-element.6) | data formatting | bytes 2359296
  104.9 0.0 copy-done
  104.9 0.7 copy.13
  105.6 0.0 copy-done.1
  105.6 0.6 copy.14
Async XLA Ops:
  102.5 2.4 %copy-start = (f32[4,48,384]{2,1,0:T(8,128)S(1)}, f32[4,48,384]{2,1,0:T(8,128)}, u32[]{:S(2)}) copy-start(f32[4,48,384]{2,1,0:T(8,128)} %get-tuple-element.7) | copy-start | bytes 884740
  102.5 3.1 %copy-start.1 = (f32[1,1536]{1,0:T(1,128)S(1)}, f32[1,1536]{1,0:T(1,128)}, u32[]{:S(2)}) copy-start(f32[1,1536]{1,0:T(1,128)} %get-tuple-element.8) | copy-start | bytes 18436

commit v4 on v3

--- a/solution.py
+++ b/solution.py
@@ -16,6 +16,7 @@
 F = 384
 Q = 4 * T
 QC = 768
+CR = 192
 MESH = pl.DeviceIdType.MESH
 BF = jnp.bfloat16
 F32 = jnp.float32
@@ -32,7 +33,7 @@
 
 
 SCRATCH = dict(
-    frames=vm(BF, T, C), cot=vm(BF, T, C), w=vm(BF, 4, C, F), taps=vm(BF, KW, C), pattern=vm(jnp.int32, 1, 6, 12),
+    frames=vm(BF, T, C), cot=vm(BF, T, C), w=vm(BF, 4, C, F), taps=vm(BF, KW, C),
     in_sem=dma(9),
     upad=vm(F32, T + 2 * HALF, C), uhalo=vm(BF, 2, HALF, C), tapsf=vm(F32, KW, C),
     bg=vm(BF, T, C), bg_t=vm(BF, C, T), frames_t=vm(BF, C, T), uh_s=dma(2), uh_r=dma(2),
@@ -88,13 +89,15 @@
         c.wait()
 
 
-def tap_terms(window, offsets):
+def correlate(acc, load, taps, offsets, rows):
     for r in range(8):
-        shifted = window[r : r + 88] if r else window
-        for a in range(5):
-            o = 8 * a + r
-            if o in offsets:
-                yield offsets[o], shifted[8 * a : 8 * a + 64]
+        part = None
+        for o in sorted(offsets):
+            if o % 8 == r:
+                term = taps(offsets[o]) * load(o - r, rows + 8 if r else rows)
+                part = term if part is None else part + term
+        acc = acc + (part[r : r + rows] if r else part)
+    return acc
 
 
 def aligned(start, size, by):
@@ -138,7 +141,6 @@
                 (w_h.at[2], s.w.at[2]),
                 (cot_h.at[0], s.cot),
                 (taps_h, s.taps),
-                (pattern_h, s.pattern),
                 (w_h.at[3], s.w.at[3]),
             ]
         )
@@ -164,9 +166,8 @@
         go(remote(s.cot.at[0:HALF], s.uhalo.at[1], s.uh_s.at[1], s.uh_r.at[1], at_tm(7))),
     ]
     load[2].wait()
-    load[6].wait()
     y = projected(s.frames[...], 0)
-    blocks = s.pattern[0]
+    blocks = pattern_h[0]
     block_of = lax.broadcasted_iota(jnp.int32, (6, T), 1) // BLK == lax.broadcasted_iota(jnp.int32, (6, T), 0)
     spread = lambda column: jnp.sum(jnp.where(block_of, column.astype(F32), 0.0), axis=0, keepdims=True)
     phase = spread(blocks[:, 0:1])
@@ -193,19 +194,25 @@
     def conv_back(it, carry):
         i, l = it // 12, lax.rem(it, 12)
         lanes = aligned(l * 128, 128, 128)
-        window = s.upad[aligned(i * 64, 96, 64), lanes]
-        acc = window[HALF : HALF + 64]
-        for j, rows in tap_terms(window, {2 * HALF - j: j for j in range(KW)}):
-            acc = acc + s.tapsf[j : j + 1, lanes] * rows
-        s.bg[aligned(i * 64, 64, 64), lanes] = acc.astype(BF)
+        base = i * CR
+        acc = correlate(
+            s.upad[aligned(base + HALF, CR, 16), lanes],
+            lambda o, n: s.upad[aligned(base + o, n, 8), lanes],
+            lambda j: s.tapsf[j : j + 1, lanes],
+            {2 * HALF - j: j for j in range(KW)},
+            CR,
+        )
+        s.bg[aligned(base, CR, CR), lanes] = acc.astype(BF)
         return carry
 
-    lax.fori_loop(0, 72, conv_back, 0)
-    load[7].wait()
+    lax.fori_loop(0, 12 * T // CR, conv_back, 0)
+    load[6].wait()
     y = projected(s.bg[...], 3)
     for h in range(4):
         s.d_s[h] = y[h * HD : (h + 1) * HD]
     d_c = [swapped(k, s.d_s.at[around(k)], s.d_r.at[x], s.ds, s.dr) for k in (1, 2, 3, 0)]
+
+    s.frames_t[...] = s.frames[...].T
 
     def forward(k, copy, buf, ssem, rsem):
         copy.wait()
@@ -315,8 +322,6 @@
         rows = aligned(lax.rem(hd + k, 4) * F, F, F)
         s.op_s[k - 1] = lax.dot_general(mixed, s.w[3, rows, :], NT, preferred_element_type=F32).astype(BF)
         op_c.append(go(remote(s.op_s.at[k - 1], s.op_r.at[k - 1], s.ops.at[k - 1], s.opr.at[k - 1], at_y(k))))
-    s.frames_t[...] = s.frames[...].T
-    s.bg_t[...] = s.bg[...].T
 
     def away(p, left, right):
         for l in range(2):
@@ -364,10 +369,8 @@
         pg_out[p] = own
 
     by_x = (False, False, True, True)
-    g3 = away(3, s.bg_t, mixed)
-
     dkv_c = []
-    for n, ks in enumerate(((1, 2), (3, 0))):
+    for ks in ((1, 2), (3, 0)):
         for slot, k in enumerate(ks):
             dk, dv = back(0, k, slot)
             p_c[k].wait()
@@ -376,11 +379,12 @@
             s.dkv_s[i, HD:] = (dv.T + s.part_r[i, HD:].astype(F32)).astype(BF)
         for k in ks:
             dkv_c.append(swapped(k, s.dkv_s.at[around(k)], s.dkv_r.at[x], s.dkvs, s.dkvr))
-        if n == 0:
-            r3 = keep(3, s.bg_t, mixed, g3, by_x[3])
     for a in range(4):
         s.dq_s[a] = (s.dq[:, a * T : (a + 1) * T] * SCALE).astype(BF)
     dq_c = [swapped(k, s.dq_s.at[around(k)], s.dq_r.at[x], s.dqs, s.dqr) for k in (1, 2, 3, 0)]
+
+    s.bg_t[...] = s.bg[...].T
+    g3 = away(3, s.bg_t, mixed)
 
     summed = lax.dot_general(mixed, s.w[3, aligned(hd * F, F, F), :], NT, preferred_element_type=F32)
     wait_all(op_c)
@@ -393,6 +397,7 @@
         go(remote(s.res.at[0:HALF], s.rhalo.at[1], s.rh_s.at[1], s.rh_r.at[1], at_tm(7))),
     ]
 
+    r3 = keep(3, s.bg_t, mixed, g3, by_x[3])
     wait_all(dkv_c)
     dk = s.dkv_r[:, 0:HD].reshape(F, T).T
     g1 = away(1, s.frames_t, dk)
@@ -404,7 +409,6 @@
     r1 = keep(1, s.frames_t, dk, g1, by_x[1])
     r2 = keep(2, s.frames_t, dv, g2, by_x[2])
     r0 = keep(0, s.frames_t, dq, g0, by_x[0])
-    t3 = second(3, r3, by_x[3])
 
     s.kacc[...] = jnp.zeros_like(s.kacc)
     s.rpad[HALF : HALF + T] = s.res[...].astype(F32)
@@ -416,16 +420,23 @@
         i, l = it // 3, lax.rem(it, 3)
         lanes = aligned(l * 128, 128, 128)
         whole = aligned(hd * F + l * 128, 128, 128)
-        window = s.rpad[aligned(i * 64, 96, 64), lanes]
-        up = s.cot[aligned(i * 64, 64, 64), whole].astype(F32)
-        acc = window[HALF : HALF + 64]
-        for j, rows in tap_terms(window, {j: j for j in range(KW)}):
-            acc = acc + s.tapsf[j : j + 1, whole] * rows
-            s.kacc[j, :, lanes] += jnp.sum((up * rows).reshape(8, 8, 128), axis=0)
-        s.enc[aligned(i * 64, 64, 64), lanes] = acc.astype(BF)
+        base = i * CR
+        window = lambda o, n: s.rpad[aligned(base + o, n, 8), lanes]
+        acc = correlate(
+            window(HALF, CR), window, lambda j: s.tapsf[j : j + 1, whole], {j: j for j in range(KW)}, CR
+        )
+        s.enc[aligned(base, CR, CR), lanes] = acc.astype(BF)
+        up = s.cot[aligned(base, CR, CR), whole].astype(F32)
+        edge = jnp.zeros((8, 128), F32)
+        up = jnp.concatenate([edge, up, edge], axis=0)
+        for r in range(8):
+            moved = up[8 - r : CR + 16 - r] if r else up[8 : CR + 8]
+            for a in range(KW // 8):
+                term = moved * window(8 * a, CR + 8 if r else CR)
+                s.kacc[8 * a + r, :, lanes] += jnp.sum(term.reshape(-1, 8, 128), axis=0)
         return carry
 
-    lax.fori_loop(0, 18, conv, 0)
+    lax.fori_loop(0, 3 * T // CR, conv, 0)
     e_c = [go(remote(s.enc, enc_out.at[0, :, mine], s.es.at[k], s.er.at[k], at_y(k))) for k in range(1, 4)]
     e_c.append(go(pltpu.make_async_copy(s.enc, enc_out.at[0, :, mine], s.in_sem.at[8])))
     for j in range(KW):
@@ -435,8 +446,9 @@
         to = lax.rem(me + k, 32)
         kg_c.append(go(remote(s.kg.at[to], s.kgr.at[k], s.kgs.at[k], s.kgrs.at[k], at_plane(k))))
 
+    t3 = second(3, r3, by_x[3])
+    t2 = second(2, r2, by_x[2])
     t1 = second(1, r1, by_x[1])
-    t2 = second(2, r2, by_x[2])
     t0 = second(0, r0, by_x[0])
     wait_all(kg_c)
     total = s.kg[me]
@@ -462,8 +474,8 @@
             jax.ShapeDtypeStruct((4, 48, F), F32),
             jax.ShapeDtypeStruct((1, C), F32),
         ),
-        in_specs=[anym] * 5,
-        out_specs=(anym, vmem, vmem),
+        in_specs=[anym, anym, anym, vmem, anym],
+        out_specs=(vmem, vmem, vmem),
         scratch_shapes=list(SCRATCH.values()),
         compiler_params=pltpu.CompilerParams(
             collective_id=0, has_side_effects=True, vmem_limit_bytes=60 << 20

time: 106 us -> 96 us (0.906)
  Pallas kernels: 101 us -> 90.1 us
    pallas_call x1, Pallas kernels: 101 us -> 90.1 us  [shards(): pl.pallas_call(layer_kernel, out_shape=(jax.ShapeDtypeStruct((1, T, C), B...]
where the time goes in v4:
time: 96 us; the launch traced here: 95.8 us
  Pallas kernels  90.1 us (94%)
  local copies, waits for them, and re-layouts  4.99 us (5%)
    pallas_call x1, Pallas kernels, shards(): pl.pallas_call(layer_kernel, out_shape=(jax.ShapeDtypeStruct((1, T, C), B...  90.1 us
    unnamed x8, local copies, waits for them, and re-layouts  4.99 us

profile of v4, /device:TPU:1, one launch (start us, length us, event | category | flops | bytes accessed | tf_op | source)
XLA Modules:
  0.0 95.8 jit_solution(5924140997714353298)
XLA Ops:
  0.6 1.3 %copy.8.pattern_h = s32[1,6,12]{2,1,0:T(8,128)} copy(s32[1,6,12]{2,0,1:T(1,128)} %param.8) | data formatting | bytes 576 | tf_op args[3]
  1.9 90.1 %conformer_layer.1 = (bf16[1,384,1536]{2,1,0:T(8,128)(2,1)}, f32[4,48,384]{2,1,0:T(8,128)}, f32[1,1536]{1,0:T(1,128)}) custom-call(bf16[1,384,1536]{2,1,0:T(8,128)(2,1)} %frames_h.1, bf16[4,1536,384]{2,1,0:T(8,128)(2,1)} %w_h.1, bf16[32,1536]{1,0:T(8,128)(2,1)} %taps_h.1, s32[1,6,12]{2,1,0:T(8,128)} %copy.8.pattern_h, bf16[1,384,1536]{2,1,0:T(8,128)(2,1)} %cot_h.1), custom_call_target="tpu_custom_call" | custom-call | tf_op jit(solution)/shard_map/conformer_layer/pallas_call | solution.py:470
  92.0 0.0 copy-start
  92.0 0.0 copy-start.1
  92.0 2.4 %copy.12 = bf16[1,384,1536]{2,1,0:T(8,128)(2,1)} copy(bf16[1,384,1536]{2,1,0:T(8,128)(2,1)} %get-tuple-element.6) | data formatting | bytes 2359296
  94.5 0.0 copy-done
  94.5 0.7 copy.13
  95.2 0.0 copy-done.1
  95.2 0.6 copy.14
Async XLA Ops:
  92.0 2.4 %copy-start = (f32[4,48,384]{2,1,0:T(8,128)S(1)}, f32[4,48,384]{2,1,0:T(8,128)}, u32[]{:S(2)}) copy-start(f32[4,48,384]{2,1,0:T(8,128)} %get-tuple-element.7) | copy-start | bytes 884740
  92.0 3.1 %copy-start.1 = (f32[1,1536]{1,0:T(1,128)S(1)}, f32[1,1536]{1,0:T(1,128)}, u32[]{:S(2)}) copy-start(f32[1,1536]{1,0:T(1,128)} %get-tuple-element.8) | copy-start | bytes 18436

commit v5 on v4

--- a/solution.py
+++ b/solution.py
@@ -21,6 +21,7 @@
 BF = jnp.bfloat16
 F32 = jnp.float32
 SCALE = HD**-0.5
+LOG2E = 1.4426950408889634
 NT = (((1,), (1,)), ((), ()))
 
 
@@ -53,9 +54,16 @@
     kacc=vm(F32, KW, 8, F), kg=vm(F32, KW, 1, F), kgr=vm(F32, KW, 1, F), kgy=vm(F32, 4, 1, F),
     kgs=dma(32), kgrs=dma(32), kys=dma(4), kyr=dma(4),
     g_s=vm(BF, 4, 2, F, F), g_r=vm(BF, 4, 2, F, F), gs=dma(4), gr=dma(4),
-    h1=vm(BF, 4, 16, 48, F), s1=vm(BF, 4, 3, 4, 48, F), h2=vm(BF, 4, 4, 48, F), s2=vm(BF, 4, 3, 48, F),
-    s1s=dma(4, 4), s1r=dma(4, 4), s2s=dma(4, 4), s2r=dma(4, 4),
+    s1s=dma(5, 4), s1r=dma(5, 4), s2s=dma(5, 4), s2r=dma(5, 4),
 )
+
+
+PARTS = ((3, 0, 48, True), (1, 0, 48, False), (2, 0, 48, True), (0, 0, 32, False), (0, 32, 16, True))
+for i, (_, _, n, _) in enumerate(PARTS):
+    SCRATCH[f"h1_{i}"] = vm(BF, 16, n, F)
+    SCRATCH[f"s1_{i}"] = vm(BF, 3, 4, n, F)
+    SCRATCH[f"h2_{i}"] = vm(BF, 4, n, F)
+    SCRATCH[f"s2_{i}"] = vm(BF, 3, n, F)
 
 
 def remote(src, dst, ssem, rsem, device):
@@ -150,8 +158,9 @@
     for device in others:
         pl.semaphore_signal(barrier, inc=1, device_id=device, device_id_type=MESH)
 
-    def projected(rows, p):
-        return jnp.dot(rows, s.w[p], preferred_element_type=F32).astype(BF).T
+    def projected(rows, p, factor=None):
+        y = jnp.dot(rows, s.w[p], preferred_element_type=F32)
+        return (y if factor is None else y * factor).astype(BF).T
 
     load[0].wait()
     load[1].wait()
@@ -166,13 +175,14 @@
         go(remote(s.cot.at[0:HALF], s.uhalo.at[1], s.uh_s.at[1], s.uh_r.at[1], at_tm(7))),
     ]
     load[2].wait()
-    y = projected(s.frames[...], 0)
-    blocks = pattern_h[0]
-    block_of = lax.broadcasted_iota(jnp.int32, (6, T), 1) // BLK == lax.broadcasted_iota(jnp.int32, (6, T), 0)
-    spread = lambda column: jnp.sum(jnp.where(block_of, column.astype(F32), 0.0), axis=0, keepdims=True)
-    phase = spread(blocks[:, 0:1])
-    count = spread(jnp.sum((blocks >= 0).astype(F32), axis=1, keepdims=True))
+    y = projected(s.frames[...], 0, SCALE * LOG2E)
     row = lax.broadcasted_iota(jnp.int32, (16, T), 0)
+    block = lax.broadcasted_iota(jnp.int32, (1, T), 1) // BLK
+    phase = count = jnp.zeros((1, T), F32)
+    for b in range(6):
+        entries = pattern_h[b]
+        phase = jnp.where(block == b, entries[:, 0:1].astype(F32), phase)
+        count = jnp.where(block == b, jnp.sum((entries >= 0).astype(F32), axis=1, keepdims=True), count)
     meta = jnp.where(row == 0, phase, jnp.where(row == 1, count, 0.0)).astype(BF)
     for h in range(4):
         s.q_s[h, 0:HD] = y[h * HD : (h + 1) * HD]
@@ -213,6 +223,7 @@
     d_c = [swapped(k, s.d_s.at[around(k)], s.d_r.at[x], s.ds, s.dr) for k in (1, 2, 3, 0)]
 
     s.frames_t[...] = s.frames[...].T
+    s.bg_t[...] = s.bg[...].T
 
     def forward(k, copy, buf, ssem, rsem):
         copy.wait()
@@ -255,23 +266,19 @@
             return top
 
         top = lax.fori_loop(0, 8, scores, jnp.full((8, QC), -jnp.inf, F32), unroll=8)
-        c2 = SCALE * 1.4426950408889634
-        top = jnp.max(top, axis=0, keepdims=True) * c2
+        top = jnp.max(top, axis=0, keepdims=True)
         if c == 0:
             wait_all(fv_c)
 
-        def weigh(t, carry):
-            total, o = carry
-            e = jnp.exp2(s.st[t] * c2 - top)
-            total = total + jnp.sum(e.reshape(T // 8, 8, QC), axis=0)
-            eb = e.astype(BF)
+        def weigh(t, o):
+            eb = jnp.exp2(s.st[t] - top).astype(BF)
             s.et[t, :, lanes] = eb
-            return total, o + jnp.dot(s.v_r[t], eb, preferred_element_type=F32)
-
-        total, o = lax.fori_loop(
-            0, 8, weigh, (jnp.zeros((8, QC), F32), jnp.zeros((HD, QC), F32)), unroll=8
-        )
-        inverse = 1.0 / jnp.sum(total, axis=0, keepdims=True)
+            values = jnp.concatenate([s.v_r[t], jnp.ones((16, T), BF)], axis=0)
+            return o + jnp.dot(values, eb, preferred_element_type=F32)
+
+        o = lax.fori_loop(0, 8, weigh, jnp.zeros((HD + 16, QC), F32), unroll=8)
+        inverse = 1.0 / o[HD : HD + 1]
+        o = o[0:HD]
         s.inverse[:, lanes] = inverse
         o = (o * inverse).astype(BF)
         for a in range(2):
@@ -297,7 +304,7 @@
             lanes = slice(c * QC, (c + 1) * QC)
             dp_ = jnp.dot(s.vn[t], s.dt[:, lanes], preferred_element_type=F32)
             s.dsb[slot, :, lanes] = (s.et[t, :, lanes].astype(F32) * (dp_ - s.delta[:, lanes])).astype(BF)
-        dk = jnp.dot(s.dsb[slot], s.qn[...], preferred_element_type=F32) * SCALE
+        dk = jnp.dot(s.dsb[slot], s.qn[...], preferred_element_type=F32) * (1 / LOG2E)
         dv = jnp.dot(s.et[t], s.dn[...], preferred_element_type=F32)
         s.dq[...] += jnp.dot(s.k_r[t], s.dsb[slot], preferred_element_type=F32)
         return dk, dv
@@ -329,46 +336,57 @@
             s.g_s[p, l] = jnp.dot(left[rows, :], right, preferred_element_type=F32).astype(BF)
         return go(remote(s.g_s.at[p], s.g_r.at[p], s.gs.at[p], s.gr.at[p], sibling))
 
-    def keep(p, left, right, copy, by_x):
+    first_c, second_c = {}, {}
+
+    def keep(p, left, right, copy):
         copy.wait()
+        parts = [(i, r0, n, by_x) for i, (q, r0, n, by_x) in enumerate(PARTS) if q == p]
         for l in range(2):
             rows = aligned((l * 2 + core) * F, F, F)
             g = jnp.dot(left[rows, :], right, preferred_element_type=F32) + s.g_r[p, l].astype(F32)
             g = g.astype(BF)
             for xo in range(4):
                 for h in range(2):
-                    piece = g[xo * 96 + h * 48 : xo * 96 + h * 48 + 48]
-                    s.h1[p, xo * 4 + h * 2 + l if by_x else (h * 2 + l) * 4 + xo] = piece
-        out = []
-        for k in range(1, 4):
-            to = lax.rem((x if by_x else z) + k, 4)
-            device = at_x(k) if by_x else at_z(k)
-            out.append(
-                go(remote(s.h1.at[p, pl.ds(to * 4, 4)], s.s1.at[p, k - 1], s.s1s.at[p, k], s.s1r.at[p, k], device))
-            )
-        return out
-
-    def second(p, copies, by_x):
-        wait_all(copies)
-        own = s.h1[p, pl.ds((x if by_x else z) * 4, 4)].astype(F32)
+                    for i, r0, n, by_x in parts:
+                        start = xo * 96 + h * 48 + r0
+                        slot = xo * 4 + h * 2 + l if by_x else (h * 2 + l) * 4 + xo
+                        getattr(s, f"h1_{i}")[slot] = g[start : start + n]
+        for i, r0, n, by_x in parts:
+            h1, s1 = getattr(s, f"h1_{i}"), getattr(s, f"s1_{i}")
+            first_c[i] = []
+            for k in range(1, 4):
+                to = lax.rem((x if by_x else z) + k, 4)
+                device = at_x(k) if by_x else at_z(k)
+                c = remote(h1.at[pl.ds(to * 4, 4)], s1.at[k - 1], s.s1s.at[i, k], s.s1r.at[i, k], device)
+                first_c[i].append(go(c))
+
+    def second(i):
+        by_x = PARTS[i][3]
+        h1, s1 = getattr(s, f"h1_{i}"), getattr(s, f"s1_{i}")
+        h2, s2 = getattr(s, f"h2_{i}"), getattr(s, f"s2_{i}")
+        wait_all(first_c[i])
+        own = h1[pl.ds((x if by_x else z) * 4, 4)].astype(F32)
         for k in range(3):
-            own = own + s.s1[p, k].astype(F32)
-        s.h2[p] = own.astype(BF)
-        out = []
+            own = own + s1[k].astype(F32)
+        h2[...] = own.astype(BF)
+        second_c[i] = []
         for k in range(1, 4):
             to = lax.rem((z if by_x else x) + k, 4)
             device = at_z(k) if by_x else at_x(k)
-            out.append(go(remote(s.h2.at[p, to], s.s2.at[p, k - 1], s.s2s.at[p, k], s.s2r.at[p, k], device)))
-        return out
-
-    def last(p, copies, by_x):
-        wait_all(copies)
-        own = s.h2[p, z if by_x else x].astype(F32)
+            c = remote(h2.at[to], s2.at[k - 1], s.s2s.at[i, k], s.s2r.at[i, k], device)
+            second_c[i].append(go(c))
+
+    def last(i):
+        p, r0, n, by_x = PARTS[i]
+        h2, s2 = getattr(s, f"h2_{i}"), getattr(s, f"s2_{i}")
+        wait_all(second_c[i])
+        own = h2[z if by_x else x].astype(F32)
         for k in range(3):
-            own = own + s.s2[p, k].astype(F32)
-        pg_out[p] = own
-
-    by_x = (False, False, True, True)
+            own = own + s2[k].astype(F32)
+        pg_out[p, r0 : r0 + n] = own
+
+    g3 = away(3, s.bg_t, mixed)
+
     dkv_c = []
     for ks in ((1, 2), (3, 0)):
         for slot, k in enumerate(ks):
@@ -379,12 +397,11 @@
             s.dkv_s[i, HD:] = (dv.T + s.part_r[i, HD:].astype(F32)).astype(BF)
         for k in ks:
             dkv_c.append(swapped(k, s.dkv_s.at[around(k)], s.dkv_r.at[x], s.dkvs, s.dkvr))
+        if ks[0] == 1:
+            keep(3, s.bg_t, mixed, g3)
     for a in range(4):
         s.dq_s[a] = (s.dq[:, a * T : (a + 1) * T] * SCALE).astype(BF)
     dq_c = [swapped(k, s.dq_s.at[around(k)], s.dq_r.at[x], s.dqs, s.dqr) for k in (1, 2, 3, 0)]
-
-    s.bg_t[...] = s.bg[...].T
-    g3 = away(3, s.bg_t, mixed)
 
     summed = lax.dot_general(mixed, s.w[3, aligned(hd * F, F, F), :], NT, preferred_element_type=F32)
     wait_all(op_c)
@@ -397,7 +414,6 @@
         go(remote(s.res.at[0:HALF], s.rhalo.at[1], s.rh_s.at[1], s.rh_r.at[1], at_tm(7))),
     ]
 
-    r3 = keep(3, s.bg_t, mixed, g3, by_x[3])
     wait_all(dkv_c)
     dk = s.dkv_r[:, 0:HD].reshape(F, T).T
     g1 = away(1, s.frames_t, dk)
@@ -406,9 +422,9 @@
     wait_all(dq_c)
     dq = s.dq_r[...].reshape(F, T).T
     g0 = away(0, s.frames_t, dq)
-    r1 = keep(1, s.frames_t, dk, g1, by_x[1])
-    r2 = keep(2, s.frames_t, dv, g2, by_x[2])
-    r0 = keep(0, s.frames_t, dq, g0, by_x[0])
+    keep(1, s.frames_t, dk, g1)
+    keep(2, s.frames_t, dv, g2)
+    keep(0, s.frames_t, dq, g0)
 
     s.kacc[...] = jnp.zeros_like(s.kacc)
     s.rpad[HALF : HALF + T] = s.res[...].astype(F32)
@@ -437,8 +453,8 @@
         return carry
 
     lax.fori_loop(0, 3 * T // CR, conv, 0)
-    e_c = [go(remote(s.enc, enc_out.at[0, :, mine], s.es.at[k], s.er.at[k], at_y(k))) for k in range(1, 4)]
-    e_c.append(go(pltpu.make_async_copy(s.enc, enc_out.at[0, :, mine], s.in_sem.at[8])))
+    e_c = [go(remote(s.enc, enc_out.at[:, mine], s.es.at[k], s.er.at[k], at_y(k))) for k in range(1, 4)]
+    e_c.append(go(pltpu.make_async_copy(s.enc, enc_out.at[:, mine], s.in_sem.at[8])))
     for j in range(KW):
         s.kg[j] = jnp.sum(s.kacc[j], axis=0, keepdims=True)
     kg_c = []
@@ -446,18 +462,16 @@
         to = lax.rem(me + k, 32)
         kg_c.append(go(remote(s.kg.at[to], s.kgr.at[k], s.kgs.at[k], s.kgrs.at[k], at_plane(k))))
 
-    t3 = second(3, r3, by_x[3])
-    t2 = second(2, r2, by_x[2])
-    t1 = second(1, r1, by_x[1])
-    t0 = second(0, r0, by_x[0])
+    for i in (0, 2, 1, 4, 3):
+        second(i)
     wait_all(kg_c)
     total = s.kg[me]
     for k in range(1, 32):
         total = total + s.kgr[k]
     s.kgy[hd] = total
     ky_c = [go(remote(s.kgy.at[hd], s.kgy.at[hd], s.kys.at[k], s.kyr.at[k], at_y(k))) for k in range(1, 4)]
-    for p, t in ((3, t3), (1, t1), (2, t2), (0, t0)):
-        last(p, t, by_x[p])
+    for i in (0, 2, 1, 4, 3):
+        last(i)
     wait_all(ky_c)
     for y in range(4):
         kg_out[:, y * F : (y + 1) * F] = s.kgy[y]
@@ -467,10 +481,10 @@
 def shards(frames, projections, kernel, pattern, cotangent):
     vmem = pl.BlockSpec(memory_space=pltpu.VMEM)
     anym = pl.BlockSpec(memory_space=pl.ANY)
-    return pl.pallas_call(
+    enc, pg, kg = pl.pallas_call(
         layer_kernel,
         out_shape=(
-            jax.ShapeDtypeStruct((1, T, C), BF),
+            jax.ShapeDtypeStruct((T, C), BF),
             jax.ShapeDtypeStruct((4, 48, F), F32),
             jax.ShapeDtypeStruct((1, C), F32),
         ),
@@ -481,7 +495,8 @@
             collective_id=0, has_side_effects=True, vmem_limit_bytes=60 << 20
         ),
         name="conformer_layer",
-    )(frames, projections, kernel, pattern, cotangent)
+    )(frames, projections, kernel, jnp.transpose(pattern, (1, 0, 2)), cotangent)
+    return enc[None], pg, kg
 
 
 def solution(mesh):

time: 96 us -> 100 us (1.042)
  Pallas kernels: 90.1 us -> 95.5 us
  local copies, waits for them, and re-layouts: 4.99 us -> 3.72 us
    pallas_call x1, Pallas kernels: 90.1 us -> 95.5 us  [shards(): pl.pallas_call(layer_kernel, out_shape=(jax.ShapeDtypeStruct((T, C), BF),...]
    unnamed x8 -> x7, local copies, waits for them, and re-layouts: 4.99 us -> 3.72 us
where the time goes in v5:
time: 100 us; the launch traced here: 99.8 us
  Pallas kernels  95.5 us (96%)
  local copies, waits for them, and re-layouts  3.72 us (4%)
    pallas_call x1, Pallas kernels, shards(): pl.pallas_call(layer_kernel, out_shape=(jax.ShapeDtypeStruct((T, C), BF),...  95.5 us
    unnamed x7, local copies, waits for them, and re-layouts  3.72 us

profile of v5, /device:TPU:1, one launch (start us, length us, event | category | flops | bytes accessed | tf_op | source)
XLA Modules:
  0.0 99.8 jit_solution(9023231849971116782)
XLA Ops:
  0.6 95.5 %conformer_layer.1 = (bf16[384,1536]{1,0:T(8,128)(2,1)}, f32[4,48,384]{2,1,0:T(8,128)}, f32[1,1536]{1,0:T(1,128)}) custom-call(bf16[1,384,1536]{2,1,0:T(8,128)(2,1)} %frames_h.1, bf16[4,1536,384]{2,1,0:T(8,128)(2,1)} %w_h.1, bf16[32,1536]{1,0:T(8,128)(2,1)} %taps_h.1, s32[6,1,12]{2,1,0:T(1,128)} %bitcast.3, bf16[1,384,1536]{2,1,0:T(8,128)(2,1)} %cot_h.1), custom_call_target="tpu_custom_call" | custom-call | tf_op jit(solution)/shard_map/conformer_layer/pallas_call | solution.py:484
  96.1 0.0 copy-start
  96.1 0.0 copy-start.1
  96.1 2.4 %copy.11 = bf16[1,384,1536]{2,1,0:T(8,128)(2,1)} copy(bf16[1,384,1536]{2,1,0:T(8,128)(2,1)} %bitcast.2) | data formatting | bytes 2359296
  98.5 0.0 copy-done
  98.5 0.7 copy.12
  99.2 0.0 copy-done.1
  99.3 0.6 copy.13
Async XLA Ops:
  96.1 2.4 %copy-start = (f32[4,48,384]{2,1,0:T(8,128)S(1)}, f32[4,48,384]{2,1,0:T(8,128)}, u32[]{:S(2)}) copy-start(f32[4,48,384]{2,1,0:T(8,128)} %get-tuple-element.13) | copy-start | bytes 884740
  96.1 3.1 %copy-start.1 = (f32[1,1536]{1,0:T(1,128)S(1)}, f32[1,1536]{1,0:T(1,128)}, u32[]{:S(2)}) copy-start(f32[1,1536]{1,0:T(1,128)} %get-tuple-element.14) | copy-start | bytes 18436

commit v6 on v5

--- a/solution.py
+++ b/solution.py
@@ -37,7 +37,7 @@
     frames=vm(BF, T, C), cot=vm(BF, T, C), w=vm(BF, 4, C, F), taps=vm(BF, KW, C),
     in_sem=dma(9),
     upad=vm(F32, T + 2 * HALF, C), uhalo=vm(BF, 2, HALF, C), tapsf=vm(F32, KW, C),
-    bg=vm(BF, T, C), bg_t=vm(BF, C, T), frames_t=vm(BF, C, T), uh_s=dma(2), uh_r=dma(2),
+    bg=vm(BF, T, C), uh_s=dma(2), uh_r=dma(2),
     q_s=vm(BF, 4, HD + 16, T), k_s=vm(BF, 4, HD, T), v_s=vm(BF, 4, HD, T), d_s=vm(BF, 4, HD, T),
     q_r=vm(BF, 4, HD + 16, T), d_r=vm(BF, 4, HD, T), k_r=vm(BF, 8, HD, T), v_r=vm(BF, 8, HD, T),
     qs=dma(4), qr=dma(4), ks=dma(4), kr=dma(4), vs=dma(4), vr=dma(4), ds=dma(4), dr=dma(4),
@@ -222,9 +222,6 @@
         s.d_s[h] = y[h * HD : (h + 1) * HD]
     d_c = [swapped(k, s.d_s.at[around(k)], s.d_r.at[x], s.ds, s.dr) for k in (1, 2, 3, 0)]
 
-    s.frames_t[...] = s.frames[...].T
-    s.bg_t[...] = s.bg[...].T
-
     def forward(k, copy, buf, ssem, rsem):
         copy.wait()
         src = lax.rem(x + 4 - k, 4)
@@ -315,12 +312,14 @@
             out[around(k), 0:HD] = dk.astype(BF).T
             out[around(k), HD:] = dv.astype(BF).T
 
-    p_c = {}
-    for ks in ((1, 2), (3, 0)):
+    def sibling_pair(ks):
         back_pair(4, ks, s.part_s)
         for k in ks:
             i = around(k)
             p_c[k] = go(remote(s.part_s.at[i], s.part_r.at[i], s.ps.at[k], s.pr.at[k], sibling))
+
+    p_c = {}
+    sibling_pair((1, 2))
 
     wait_all(o_c)
     mixed = s.mix_r[...].reshape(F, T).T
@@ -329,6 +328,8 @@
         rows = aligned(lax.rem(hd + k, 4) * F, F, F)
         s.op_s[k - 1] = lax.dot_general(mixed, s.w[3, rows, :], NT, preferred_element_type=F32).astype(BF)
         op_c.append(go(remote(s.op_s.at[k - 1], s.op_r.at[k - 1], s.ops.at[k - 1], s.opr.at[k - 1], at_y(k))))
+
+    sibling_pair((3, 0))
 
     def away(p, left, right):
         for l in range(2):
@@ -385,8 +386,6 @@
             own = own + s2[k].astype(F32)
         pg_out[p, r0 : r0 + n] = own
 
-    g3 = away(3, s.bg_t, mixed)
-
     dkv_c = []
     for ks in ((1, 2), (3, 0)):
         for slot, k in enumerate(ks):
@@ -397,8 +396,6 @@
             s.dkv_s[i, HD:] = (dv.T + s.part_r[i, HD:].astype(F32)).astype(BF)
         for k in ks:
             dkv_c.append(swapped(k, s.dkv_s.at[around(k)], s.dkv_r.at[x], s.dkvs, s.dkvr))
-        if ks[0] == 1:
-            keep(3, s.bg_t, mixed, g3)
     for a in range(4):
         s.dq_s[a] = (s.dq[:, a * T : (a + 1) * T] * SCALE).astype(BF)
     dq_c = [swapped(k, s.dq_s.at[around(k)], s.dq_r.at[x], s.dqs, s.dqr) for k in (1, 2, 3, 0)]
@@ -414,19 +411,10 @@
         go(remote(s.res.at[0:HALF], s.rhalo.at[1], s.rh_s.at[1], s.rh_r.at[1], at_tm(7))),
     ]
 
-    wait_all(dkv_c)
-    dk = s.dkv_r[:, 0:HD].reshape(F, T).T
-    g1 = away(1, s.frames_t, dk)
-    dv = s.dkv_r[:, HD:].reshape(F, T).T
-    g2 = away(2, s.frames_t, dv)
-    wait_all(dq_c)
-    dq = s.dq_r[...].reshape(F, T).T
-    g0 = away(0, s.frames_t, dq)
-    keep(1, s.frames_t, dk, g1)
-    keep(2, s.frames_t, dv, g2)
-    keep(0, s.frames_t, dq, g0)
-
-    s.kacc[...] = jnp.zeros_like(s.kacc)
+    bg_t, frames_t = s.w.at[0], s.w.at[1]
+    bg_t[...] = s.bg[...].T
+    g3 = away(3, bg_t, mixed)
+
     s.rpad[HALF : HALF + T] = s.res[...].astype(F32)
     wait_all(halos)
     s.rpad[0:HALF] = jnp.where(tm > 0, s.rhalo[0].astype(F32), 0.0)
@@ -442,19 +430,42 @@
             window(HALF, CR), window, lambda j: s.tapsf[j : j + 1, whole], {j: j for j in range(KW)}, CR
         )
         s.enc[aligned(base, CR, CR), lanes] = acc.astype(BF)
-        up = s.cot[aligned(base, CR, CR), whole].astype(F32)
+        return carry
+
+    lax.fori_loop(0, 3 * T // CR, conv, 0)
+    e_c = [go(remote(s.enc, enc_out.at[:, mine], s.es.at[k], s.er.at[k], at_y(k))) for k in range(1, 4)]
+    e_c.append(go(pltpu.make_async_copy(s.enc, enc_out.at[:, mine], s.in_sem.at[8])))
+    keep(3, bg_t, mixed, g3)
+    frames_t[...] = s.frames[...].T
+    wait_all(dkv_c)
+    dk = s.dkv_r[:, 0:HD].reshape(F, T).T
+    g1 = away(1, frames_t, dk)
+    dv = s.dkv_r[:, HD:].reshape(F, T).T
+    g2 = away(2, frames_t, dv)
+    wait_all(dq_c)
+    dq = s.dq_r[...].reshape(F, T).T
+    g0 = away(0, frames_t, dq)
+    keep(1, frames_t, dk, g1)
+    keep(2, frames_t, dv, g2)
+    keep(0, frames_t, dq, g0)
+
+    s.kacc[...] = jnp.zeros_like(s.kacc)
+
+    def taps_grad(it, carry):
+        i, l = it // 3, lax.rem(it, 3)
+        lanes = aligned(l * 128, 128, 128)
+        base = i * CR
+        up = s.cot[aligned(base, CR, CR), aligned(hd * F + l * 128, 128, 128)].astype(F32)
         edge = jnp.zeros((8, 128), F32)
         up = jnp.concatenate([edge, up, edge], axis=0)
         for r in range(8):
             moved = up[8 - r : CR + 16 - r] if r else up[8 : CR + 8]
             for a in range(KW // 8):
-                term = moved * window(8 * a, CR + 8 if r else CR)
+                term = moved * s.rpad[aligned(base + 8 * a, CR + 8 if r else CR, 8), lanes]
                 s.kacc[8 * a + r, :, lanes] += jnp.sum(term.reshape(-1, 8, 128), axis=0)
         return carry
 
-    lax.fori_loop(0, 3 * T // CR, conv, 0)
-    e_c = [go(remote(s.enc, enc_out.at[:, mine], s.es.at[k], s.er.at[k], at_y(k))) for k in range(1, 4)]
-    e_c.append(go(pltpu.make_async_copy(s.enc, enc_out.at[:, mine], s.in_sem.at[8])))
+    lax.fori_loop(0, 3 * T // CR, taps_grad, 0)
     for j in range(KW):
         s.kg[j] = jnp.sum(s.kacc[j], axis=0, keepdims=True)
     kg_c = []
@@ -489,10 +500,10 @@
             jax.ShapeDtypeStruct((1, C), F32),
         ),
         in_specs=[anym, anym, anym, vmem, anym],
-        out_specs=(vmem, vmem, vmem),
+        out_specs=(anym, vmem, vmem),
         scratch_shapes=list(SCRATCH.values()),
         compiler_params=pltpu.CompilerParams(
-            collective_id=0, has_side_effects=True, vmem_limit_bytes=60 << 20
+            collective_id=0, has_side_effects=True, vmem_limit_bytes=55 << 20
         ),
         name="conformer_layer",
     )(frames, projections, kernel, jnp.transpose(pattern, (1, 0, 2)), cotangent)

time: 100 us -> 96.4 us (0.964)
  Pallas kernels: 95.5 us -> 91.8 us
    pallas_call x1, Pallas kernels: 95.5 us -> 91.8 us  [shards(): pl.pallas_call(layer_kernel, out_shape=(jax.ShapeDtypeStruct((T, C), BF),...]
where the time goes in v6:
time: 96.4 us; the launch traced here: 96.2 us
  Pallas kernels  91.8 us (95%)
  local copies, waits for them, and re-layouts  3.72 us (4%)
    pallas_call x1, Pallas kernels, shards(): pl.pallas_call(layer_kernel, out_shape=(jax.ShapeDtypeStruct((T, C), BF),...  91.8 us
    unnamed x7, local copies, waits for them, and re-layouts  3.72 us

profile of v6, /device:TPU:1, one launch (start us, length us, event | category | flops | bytes accessed | tf_op | source)
XLA Modules:
  0.0 96.2 jit_solution(7560258660006926206)
XLA Ops:
  0.6 91.8 %conformer_layer.1 = (bf16[384,1536]{1,0:T(8,128)(2,1)}, f32[4,48,384]{2,1,0:T(8,128)}, f32[1,1536]{1,0:T(1,128)}) custom-call(bf16[1,384,1536]{2,1,0:T(8,128)(2,1)} %frames_h.1, bf16[4,1536,384]{2,1,0:T(8,128)(2,1)} %w_h.1, bf16[32,1536]{1,0:T(8,128)(2,1)} %taps_h.1, s32[6,1,12]{2,1,0:T(1,128)} %bitcast.3, bf16[1,384,1536]{2,1,0:T(8,128)(2,1)} %cot_h.1), custom_call_target="tpu_custom_call" | custom-call | tf_op jit(solution)/shard_map/conformer_layer/pallas_call | solution.py:495
  92.5 0.0 copy-start
  92.5 0.0 copy-start.1
  92.5 2.4 %copy.11 = bf16[1,384,1536]{2,1,0:T(8,128)(2,1)} copy(bf16[1,384,1536]{2,1,0:T(8,128)(2,1)} %bitcast.2) | data formatting | bytes 2359296
  94.9 0.0 copy-done
  94.9 0.7 copy.12
  95.6 0.0 copy-done.1
  95.6 0.6 copy.13
Async XLA Ops:
  92.5 2.4 %copy-start = (f32[4,48,384]{2,1,0:T(8,128)S(1)}, f32[4,48,384]{2,1,0:T(8,128)}, u32[]{:S(2)}) copy-start(f32[4,48,384]{2,1,0:T(8,128)} %get-tuple-element.13) | copy-start | bytes 884740
  92.5 3.1 %copy-start.1 = (f32[1,1536]{1,0:T(1,128)S(1)}, f32[1,1536]{1,0:T(1,128)}, u32[]{:S(2)}) copy-start(f32[1,1536]{1,0:T(1,128)} %get-tuple-element.14) | copy-start | bytes 18436

commit v7 on v6

--- a/solution.py
+++ b/solution.py
@@ -168,12 +168,12 @@
     for h in range(4):
         s.k_s[h] = y[h * HD : (h + 1) * HD]
     pl.semaphore_wait(barrier, len(others))
-    k_c = [swapped(k, s.k_s.at[around(k)], s.k_r.at[x], s.ks, s.kr) for k in (1, 2, 3, 0)]
     load[4].wait()
     halos = [
         go(remote(s.cot.at[T - HALF : T], s.uhalo.at[0], s.uh_s.at[0], s.uh_r.at[0], at_tm(1))),
         go(remote(s.cot.at[0:HALF], s.uhalo.at[1], s.uh_s.at[1], s.uh_r.at[1], at_tm(7))),
     ]
+    k_c = [swapped(k, s.k_s.at[around(k)], s.k_r.at[x], s.ks, s.kr) for k in (1, 2, 3, 0)]
     load[2].wait()
     y = projected(s.frames[...], 0, SCALE * LOG2E)
     row = lax.broadcasted_iota(jnp.int32, (16, T), 0)
@@ -415,26 +415,6 @@
     bg_t[...] = s.bg[...].T
     g3 = away(3, bg_t, mixed)
 
-    s.rpad[HALF : HALF + T] = s.res[...].astype(F32)
-    wait_all(halos)
-    s.rpad[0:HALF] = jnp.where(tm > 0, s.rhalo[0].astype(F32), 0.0)
-    s.rpad[HALF + T :] = jnp.where(tm < 7, s.rhalo[1].astype(F32), 0.0)
-
-    def conv(it, carry):
-        i, l = it // 3, lax.rem(it, 3)
-        lanes = aligned(l * 128, 128, 128)
-        whole = aligned(hd * F + l * 128, 128, 128)
-        base = i * CR
-        window = lambda o, n: s.rpad[aligned(base + o, n, 8), lanes]
-        acc = correlate(
-            window(HALF, CR), window, lambda j: s.tapsf[j : j + 1, whole], {j: j for j in range(KW)}, CR
-        )
-        s.enc[aligned(base, CR, CR), lanes] = acc.astype(BF)
-        return carry
-
-    lax.fori_loop(0, 3 * T // CR, conv, 0)
-    e_c = [go(remote(s.enc, enc_out.at[:, mine], s.es.at[k], s.er.at[k], at_y(k))) for k in range(1, 4)]
-    e_c.append(go(pltpu.make_async_copy(s.enc, enc_out.at[:, mine], s.in_sem.at[8])))
     keep(3, bg_t, mixed, g3)
     frames_t[...] = s.frames[...].T
     wait_all(dkv_c)
@@ -448,6 +428,27 @@
     keep(1, frames_t, dk, g1)
     keep(2, frames_t, dv, g2)
     keep(0, frames_t, dq, g0)
+
+    s.rpad[HALF : HALF + T] = s.res[...].astype(F32)
+    wait_all(halos)
+    s.rpad[0:HALF] = jnp.where(tm > 0, s.rhalo[0].astype(F32), 0.0)
+    s.rpad[HALF + T :] = jnp.where(tm < 7, s.rhalo[1].astype(F32), 0.0)
+
+    def conv(it, carry):
+        i, l = it // 3, lax.rem(it, 3)
+        lanes = aligned(l * 128, 128, 128)
+        whole = aligned(hd * F + l * 128, 128, 128)
+        base = i * CR
+        window = lambda o, n: s.rpad[aligned(base + o, n, 8), lanes]
+        acc = correlate(
+            window(HALF, CR), window, lambda j: s.tapsf[j : j + 1, whole], {j: j for j in range(KW)}, CR
+        )
+        s.enc[aligned(base, CR, CR), lanes] = acc.astype(BF)
+        return carry
+
+    lax.fori_loop(0, 3 * T // CR, conv, 0)
+    e_c = [go(remote(s.enc, enc_out.at[:, mine], s.es.at[k], s.er.at[k], at_y(k))) for k in range(1, 4)]
+    e_c.append(go(pltpu.make_async_copy(s.enc, enc_out.at[:, mine], s.in_sem.at[8])))
 
     s.kacc[...] = jnp.zeros_like(s.kacc)
 

time: 96.4 us -> 92.6 us (0.961)
  Pallas kernels: 91.8 us -> 88 us
    pallas_call x1, Pallas kernels: 91.8 us -> 88 us  [shards(): pl.pallas_call(layer_kernel, out_shape=(jax.ShapeDtypeStruct((T, C), BF),...]
where the time goes in v7:
time: 92.6 us; the launch traced here: 92.4 us
  Pallas kernels  88 us (95%)
  local copies, waits for them, and re-layouts  3.72 us (4%)
    pallas_call x1, Pallas kernels, shards(): pl.pallas_call(layer_kernel, out_shape=(jax.ShapeDtypeStruct((T, C), BF),...  88 us
    unnamed x7, local copies, waits for them, and re-layouts  3.72 us

profile of v7, /device:TPU:1, one launch (start us, length us, event | category | flops | bytes accessed | tf_op | source)
XLA Modules:
  0.0 92.4 jit_solution(9030570854980066048)
XLA Ops:
  0.6 88.0 %conformer_layer.1 = (bf16[384,1536]{1,0:T(8,128)(2,1)}, f32[4,48,384]{2,1,0:T(8,128)}, f32[1,1536]{1,0:T(1,128)}) custom-call(bf16[1,384,1536]{2,1,0:T(8,128)(2,1)} %frames_h.1, bf16[4,1536,384]{2,1,0:T(8,128)(2,1)} %w_h.1, bf16[32,1536]{1,0:T(8,128)(2,1)} %taps_h.1, s32[6,1,12]{2,1,0:T(1,128)} %bitcast.3, bf16[1,384,1536]{2,1,0:T(8,128)(2,1)} %cot_h.1), custom_call_target="tpu_custom_call" | custom-call | tf_op jit(solution)/shard_map/conformer_layer/pallas_call | solution.py:496
  88.7 0.0 copy-start
  88.7 0.0 copy-start.1
  88.7 2.4 %copy.11 = bf16[1,384,1536]{2,1,0:T(8,128)(2,1)} copy(bf16[1,384,1536]{2,1,0:T(8,128)(2,1)} %bitcast.2) | data formatting | bytes 2359296
  91.1 0.0 copy-done
  91.1 0.7 copy.12
  91.8 0.0 copy-done.1
  91.8 0.6 copy.13
Async XLA Ops:
  88.7 2.4 %copy-start = (f32[4,48,384]{2,1,0:T(8,128)S(1)}, f32[4,48,384]{2,1,0:T(8,128)}, u32[]{:S(2)}) copy-start(f32[4,48,384]{2,1,0:T(8,128)} %get-tuple-element.13) | copy-start | bytes 884740
  88.7 3.1 %copy-start.1 = (f32[1,1536]{1,0:T(1,128)S(1)}, f32[1,1536]{1,0:T(1,128)}, u32[]{:S(2)}) copy-start(f32[1,1536]{1,0:T(1,128)} %get-tuple-element.14) | copy-start | bytes 18436

commit v8 on v7

--- a/solution.py
+++ b/solution.py
@@ -321,6 +321,8 @@
     p_c = {}
     sibling_pair((1, 2))
 
+    sibling_pair((3, 0))
+
     wait_all(o_c)
     mixed = s.mix_r[...].reshape(F, T).T
     op_c = []
@@ -329,7 +331,6 @@
         s.op_s[k - 1] = lax.dot_general(mixed, s.w[3, rows, :], NT, preferred_element_type=F32).astype(BF)
         op_c.append(go(remote(s.op_s.at[k - 1], s.op_r.at[k - 1], s.ops.at[k - 1], s.opr.at[k - 1], at_y(k))))
 
-    sibling_pair((3, 0))
 
     def away(p, left, right):
         for l in range(2):

time: 92.6 us -> 91.7 us (level)
    pallas_call x1, Pallas kernels: 88 us -> 87.1 us  [shards(): pl.pallas_call(layer_kernel, out_shape=(jax.ShapeDtypeStruct((T, C), BF),...]
where the time goes in v8:
time: 91.7 us; the launch traced here: 91.4 us
  Pallas kernels  87.1 us (95%)
  local copies, waits for them, and re-layouts  3.72 us (4%)
    pallas_call x1, Pallas kernels, shards(): pl.pallas_call(layer_kernel, out_shape=(jax.ShapeDtypeStruct((T, C), BF),...  87.1 us
    unnamed x7, local copies, waits for them, and re-layouts  3.72 us

profile of v8, /device:TPU:1, one launch (start us, length us, event | category | flops | bytes accessed | tf_op | source)
XLA Modules:
  0.0 91.4 jit_solution(14064536695197818630)
XLA Ops:
  0.6 87.1 %conformer_layer.1 = (bf16[384,1536]{1,0:T(8,128)(2,1)}, f32[4,48,384]{2,1,0:T(8,128)}, f32[1,1536]{1,0:T(1,128)}) custom-call(bf16[1,384,1536]{2,1,0:T(8,128)(2,1)} %frames_h.1, bf16[4,1536,384]{2,1,0:T(8,128)(2,1)} %w_h.1, bf16[32,1536]{1,0:T(8,128)(2,1)} %taps_h.1, s32[6,1,12]{2,1,0:T(1,128)} %bitcast.3, bf16[1,384,1536]{2,1,0:T(8,128)(2,1)} %cot_h.1), custom_call_target="tpu_custom_call" | custom-call | tf_op jit(solution)/shard_map/conformer_layer/pallas_call | solution.py:497
  87.7 0.0 copy-start
  87.7 0.0 copy-start.1
  87.7 2.4 %copy.11 = bf16[1,384,1536]{2,1,0:T(8,128)(2,1)} copy(bf16[1,384,1536]{2,1,0:T(8,128)(2,1)} %bitcast.2) | data formatting | bytes 2359296
  90.1 0.0 copy-done
  90.1 0.7 copy.12
  90.8 0.0 copy-done.1
  90.8 0.6 copy.13
Async XLA Ops:
  87.7 2.4 %copy-start = (f32[4,48,384]{2,1,0:T(8,128)S(1)}, f32[4,48,384]{2,1,0:T(8,128)}, u32[]{:S(2)}) copy-start(f32[4,48,384]{2,1,0:T(8,128)} %get-tuple-element.13) | copy-start | bytes 884740
  87.7 3.1 %copy-start.1 = (f32[1,1536]{1,0:T(1,128)S(1)}, f32[1,1536]{1,0:T(1,128)}, u32[]{:S(2)}) copy-start(f32[1,1536]{1,0:T(1,128)} %get-tuple-element.14) | copy-start | bytes 18436
